TPU v7x, 128 devices: a whole 4x4x4 slice. The times are simulated.
128 devices in a mesh: row: 16 (over y_lo, x, core), col: 8 (over y_hi, z).
Axes of the slice: x: 4, y: 4 (y_hi: 2, y_lo: 2; y = y_hi * 2 + y_lo), z: 4, core: 2. Of those that a mesh axis runs over, the one named last changes fastest.
Arguments:
- gradient: float32 [5120, 9216], P('row', 'col'), may hold values from -0.015625 to 0.015625
- momentum: float32 [5120, 9216], P('row', 'col'), may hold values from -0.015625 to 0.015625
Outputs:
- new_momentum: float32 [5120, 9216], P('row', 'col')
- update: float32 [5120, 9216], P('row', 'col')
All inputs are finite; a program needn't handle non-finite values.
Results may differ from a plain program's by a relative error of at most 0.013.
Values may be sent and summed in bfloat16 or wider, within the bound.
A program may use at most 128 MiB of HBM per device.

v0:
```python
import math

import jax
import jax.numpy as jnp
from jax import lax
from jax.sharding import PartitionSpec as P

HIDDEN_SIZE = 9216


MOMENTUM_RATE = 0.95
COEF_A = 3.4445
COEF_B = -4.775
COEF_C = 2.0315


def local(gradient, momentum):
    new_momentum = MOMENTUM_RATE * momentum + gradient
    nesterov = gradient + MOMENTUM_RATE * new_momentum
    lowered = nesterov.astype(jnp.bfloat16)
    contract_last = (((1,), (1,)), ((), ()))
    x_slab = lax.all_gather(lowered, "row", axis=0, tiled=True)
    partial_value = lax.dot_general(
        lowered, x_slab, contract_last, preferred_element_type=jnp.float32
    )
    gram_block = lax.psum_scatter(
        partial_value.astype(jnp.bfloat16), "col", scatter_dimension=1, tiled=True
    ).astype(jnp.float32)
    gram_half = gram_block.astype(jnp.bfloat16)
    gram_panel = lax.all_gather(gram_half, "col", axis=1, tiled=True)
    square = jnp.dot(
        gram_panel,
        lax.all_gather(gram_half, "row", axis=0, tiled=True),
        preferred_element_type=jnp.float32,
    )
    mixing = (COEF_B * gram_block + COEF_C * square).astype(jnp.bfloat16)
    product = jnp.dot(
        lax.all_gather(mixing, "col", axis=1, tiled=True),
        x_slab,
        preferred_element_type=jnp.float32,
    )
    update = math.sqrt(HIDDEN_SIZE) * (COEF_A * nesterov + product)
    return (new_momentum, update)


def solution(mesh):
    in_specs = (P("row", "col"), P("row", "col"))
    out_specs = (P("row", "col"), P("row", "col"))
    return jax.shard_map(local, mesh=mesh, in_specs=in_specs, out_specs=out_specs, check_vma=False)
```

profile of v0, /device:TPU:1, one launch (start us, length us, event | category | flops | bytes accessed | tf_op | source)
XLA Modules:
  0.0 377.9 jit_solution(15078235878229540443)
XLA Ops:
  7.2 0.0 all-gather.5.cloned.1.call-start
  7.2 3.4 fusion.3
  10.6 0.0 all-gather.5.cloned.1.call-update
  10.6 0.0 reduce-scatter.4.cloned.1.call-start
  10.7 71.9 %all-gather.5.cloned.1.call-done = bf16[5120,1152]{1,0:T(8,128)(2,1)} async-done(((bf16[320,1152]{1,0:T(8,128)(2,1)}), bf16[5120,1152]{1,0:T(8,128)(2,1)}) %all-gather.5.cloned.1.call-update) | async-done | bytes 11796496 | tf_op jit(solution)/shard_map/all_gather | solution.py:22
  82.6 9.0 %convolution_convert_fusion = bf16[320,5120]{1,0:T(8,128)(2,1)S(1)} fusion(bf16[320,1152]{1,0:T(8,128)(2,1)} %get-tuple-element.2, bf16[5120,1152]{1,0:T(8,128)(2,1)} %all-gather.5.cloned.1.call-done), kind=kOutput, calls=%fused_computation | convolution fusion | flops 3776512000 | bytes 15810560 | tf_op jit(solution)/shard_map/dot_general | solution.py:23
  91.6 3.7 copy.4
  95.3 0.0 reduce-scatter.4.cloned.1.call-update
  95.3 0.0 all-gather.7.cloned.1.call-start
  95.3 82.9 %reduce-scatter.4.cloned.1.call-done = bf16[640,320]{1,0:T(8,128)(2,1)} async-done(((bf16[5120,320]{1,0:T(8,128)(2,1)}), bf16[640,320]{1,0:T(8,128)(2,1)}) %reduce-scatter.4.cloned.1.call-update) | async-done | bytes 409616
  178.2 2.0 copy.5
  180.2 0.0 all-gather.7.cloned.1.call-update
  180.2 0.0 all-gather.9.cloned.1.call-start
  180.2 0.5 all-gather.9.cloned.1.call-update
  180.8 0.0 copy-start
  180.8 0.0 copy-start.1
  180.8 0.0 all-gather.11.cloned.1.call-start
  180.8 64.1 %all-gather.7.cloned.1.call-done = bf16[320,5120]{1,0:T(8,128)(2,1)} async-done(((bf16[320,640]{1,0:T(8,128)(2,1)}), bf16[320,5120]{1,0:T(8,128)(2,1)}) %all-gather.7.cloned.1.call-update) | async-done | bytes 3276816 | tf_op jit(solution)/shard_map/all_gather | solution.py:30
  244.9 44.3 %all-gather.9.cloned.1.call-done = bf16[5120,640]{1,0:T(8,128)(2,1)} async-done(((bf16[320,640]{1,0:T(8,128)(2,1)}), bf16[5120,640]{1,0:T(8,128)(2,1)}) %all-gather.9.cloned.1.call-update) | async-done | bytes 6553616 | tf_op jit(solution)/shard_map/all_gather | solution.py:33
  289.2 7.3 %fusion.2 = bf16[320,640]{1,0:T(8,128)(2,1)} fusion(bf16[320,5120]{1,0:T(8,128)(2,1)} %all-gather.7.cloned.1.call-done, bf16[5120,640]{1,0:T(8,128)(2,1)} %all-gather.9.cloned.1.call-done, bf16[320,640]{1,0:T(8,128)(2,1)} %copy.5), kind=kOutput, calls=%fused_computation.7 | convolution fusion | flops 2098176000 | bytes 10649600 | tf_op jit(solution)/shard_map/dot_general | solution.py:31
  296.5 0.0 all-gather.11.cloned.1.call-update
  296.5 64.0 %all-gather.11.cloned.1.call-done = bf16[320,5120]{1,0:T(8,128)(2,1)} async-done(((bf16[320,640]{1,0:T(8,128)(2,1)}), bf16[320,5120]{1,0:T(8,128)(2,1)}) %all-gather.11.cloned.1.call-update) | async-done | bytes 3276816 | tf_op jit(solution)/shard_map/all_gather | solution.py:38
  360.5 0.0 copy-done
  360.5 10.9 %fusion = f32[320,1152]{1,0:T(8,128)} fusion(bf16[320,5120]{1,0:T(8,128)(2,1)} %all-gather.11.cloned.1.call-done, bf16[5120,1152]{1,0:T(8,128)(2,1)} %all-gather.5.cloned.1.call-done, f32[320,1152]{1,0:T(8,128)S(1)} %copy-done, f32[320,1152]{1,0:T(8,128)S(1)} %copy-done.1), kind=kOutput, calls=%fused_computation.2 | convolution fusion | flops 3776716800 | bytes 19496960 | tf_op jit(solution)/shard_map/dot_general | solution.py:37
  (1 shorter events, 0.0 us)
Async XLA Ops:
  7.2 75.4 %all-gather.5.cloned.1.call-start = ((), (), s32[]{:S(2)}) async-start(), calls=%async_computation.1 | async-start | bytes 12533760 | tf_op jit(solution)/shard_map/all_gather | solution.py:22
  10.6 167.5 %reduce-scatter.4.cloned.1.call-start = ((), (), s32[]{:S(2)}) async-start(), calls=%async_computation.5 | async-start | bytes 4423680
  95.3 149.6 %all-gather.7.cloned.1.call-start = ((), (), s32[]{:S(2)}) async-start(), calls=%async_computation.2 | async-start | bytes 3686400 | tf_op jit(solution)/shard_map/all_gather | solution.py:30
  180.2 109.0 %all-gather.9.cloned.1.call-start = ((), (), s32[]{:S(2)}) async-start(), calls=%async_computation.3 | async-start | bytes 6963200 | tf_op jit(solution)/shard_map/all_gather | solution.py:33
  180.8 179.7 %copy-start = (f32[320,1152]{1,0:T(8,128)S(1)}, f32[320,1152]{1,0:T(8,128)}, u32[]{:S(2)}) copy-start(f32[320,1152]{1,0:T(8,128)} %param.2) | copy-start | bytes 4423684
  180.8 179.7 %copy-start.1 = (f32[320,1152]{1,0:T(8,128)S(1)}, f32[320,1152]{1,0:T(8,128)}, u32[]{:S(2)}) copy-start(f32[320,1152]{1,0:T(8,128)} %get-tuple-element.3) | copy-start | bytes 4423684
  180.8 179.7 %all-gather.11.cloned.1.call-start = ((), (), s32[]{:S(2)}) async-start(), calls=%async_computation.4 | async-start | bytes 3686400 | tf_op jit(solution)/shard_map/all_gather | solution.py:38
Sparse Core Ops, SparseCore 0:
  10.8 71.7 all-gather.4
  95.4 82.7 reduce-scatter.3
  181.5 63.4 all-gather.6
  247.2 41.9 all-gather.8
  296.6 63.8 all-gather.10
where the time goes:
time: 378 us
  waiting for transfers between devices  328 us (87%)
  matrix products  27.2 us (7%)
  between operations  13.8 us (4%)
  local copies, waits for them, and re-layouts  5.63 us (1%)
    unnamed x6, waiting for transfers between devices  83.4 us
    all_gather x1, waiting for transfers between devices, local(): x_slab = lax.all_gather(lowered, 'row', axis=0, tiled=True)  71.9 us
    all_gather x1, waiting for transfers between devices, local(): gram_panel = lax.all_gather(gram_half, 'col', axis=1, tiled=True)  64.1 us
    all_gather x1, waiting for transfers between devices, local(): lax.all_gather(mixing, 'col', axis=1, tiled=True)  64 us
    all_gather x1, waiting for transfers between devices, local(): lax.all_gather(gram_half, 'row', axis=0, tiled=True)  44.3 us
    dot_general x1, matrix products, local(): jnp.dot(lax.all_gather(mixing, 'col', axis=1, tiled=True), x_slab, prefer...  10.9 us
    dot_general x1, matrix products, local(): lax.dot_general(lowered, x_slab, contract_last, preferred_element_type=jn...  9.02 us
  transfers between devices with their start and end apart: 5, of which 5 were waited for; matrix products, arithmetic and copies ran while one was open for 0% of the time, Pallas kernels for 0%

commit v1 on v0

v1 whole, which is shorter than its diff:
```python
import math

import jax
import jax.numpy as jnp
from jax import lax
from jax.experimental import pallas as pl
from jax.experimental.pallas import tpu as pltpu
from jax.sharding import PartitionSpec as P

HIDDEN_SIZE = 9216
MOMENTUM_RATE = 0.95
COEF_A = 3.4445
COEF_B = -4.775
COEF_C = 2.0315
SCALE = math.sqrt(HIDDEN_SIZE)

MESH = pl.DeviceIdType.MESH
ROWS = 320
COLS = 1152
HALF = ROWS // 2
CHIP = 2 * ROWS
PIECE = ROWS // 4
PLACES = {(0, 0): 0, (-1, 0): 1, (1, 0): 2, (2, 0): 3, (0, 1): 4, (-1, 1): 5, (1, 1): 6, (2, 1): 7}


class Gather:
    def __init__(self, slot, plus, minus, pair, send, recv, over_pair):
        self.slot, self.plus, self.minus, self.pair = slot, plus, minus, pair
        self.send, self.recv, self.over_pair, self.started = send, recv, over_pair, []

    def _copy(self, dr, dp, h, to):
        device, ring, other = {"plus": (self.plus, -1, 0), "minus": (self.minus, 1, 0), "pair": (self.pair, 0, 1)}[to]
        there = dr + ring
        there = 2 if there == -2 else there
        place = PLACES[(there, (dp + other) % 2)] * 2 + h
        ref = self.slot(dr, dp, h)
        copy = pltpu.make_async_remote_copy(
            src_ref=ref,
            dst_ref=ref,
            send_sem=self.send.at[len(self.started)],
            recv_sem=self.recv.at[place],
            device_id=device,
            device_id_type=MESH,
        )
        copy.start()
        self.started.append(copy)

    def begin(self, h):
        for to in ("plus", "minus", "pair"):
            self._copy(0, 0, h, to)

    def arrive(self, dr, dp, h):
        ref = self.slot(dr, dp, h)
        place = PLACES[(dr, dp)] * 2 + h
        pltpu.make_async_remote_copy(
            src_ref=ref,
            dst_ref=ref,
            send_sem=self.send.at[0],
            recv_sem=self.recv.at[place],
            device_id=self.pair,
            device_id_type=MESH,
        ).wait_recv()
        if (dr, dp) == (0, 1):
            self._copy(dr, dp, h, "plus")
            self._copy(dr, dp, h, "minus")
        elif (dr, dp, h) == (-1, 0, 0) or (dr, dp, h, self.over_pair) == (-1, 1, 0, False):
            self._copy(dr, dp, h, "plus")
        elif (dr, dp, h) == (1, 0, 1) or (dr, dp, h, self.over_pair) == (1, 1, 1, False):
            self._copy(dr, dp, h, "minus")
        elif (dr, dp) == (2, 0) and self.over_pair:
            self._copy(dr, dp, h, "pair")

    def finish(self):
        for copy in self.started:
            copy.wait_send()


def kernel(
    g_ref, m_ref, nm_ref, up_ref,
    xs, xi, xt, ps, r1, keep, s_send, s_recv, gf, rt, ls, ms, mt, zs, zr,
    x_send, x_recv, xc_send, xc_recv, r1_send, r1_recv, r2_send, r2_recv,
    rt_send, rt_recv, l_send, l_recv, lc_send, lc_recv, m_send, m_recv, z_send, z_recv,
):
    row, col = lax.axis_index("row"), lax.axis_index("col")
    c, x, yl = row % 2, (row // 2) % 4, row // 8
    z, yh = col % 4, col // 4

    def device(x_, yl_, c_, yh_, z_):
        return ((yl_ * 4 + x_) * 2 + c_, yh_ * 4 + z_)

    core = device(x, yl, 1 - c, yh, z)
    xp, xm = device((x + 1) % 4, yl, c, yh, z), device((x + 3) % 4, yl, c, yh, z)
    zp, zm = device(x, yl, c, yh, (z + 1) % 4), device(x, yl, c, yh, (z + 3) % 4)
    z2 = device(x, yl, c, yh, (z + 2) % 4)
    yp, yq = device(x, 1 - yl, c, yh, z), device(x, yl, c, 1 - yh, z)
    barrier = pltpu.get_barrier_semaphore()
    partners = (core, xp, xm, zp, zm, z2, yp, yq)
    for partner in partners:
        pl.semaphore_signal(barrier, inc=1, device_id=partner, device_id_type=MESH)

    def remote(src, dst, send, recv, to):
        return pltpu.make_async_remote_copy(
            src_ref=src, dst_ref=dst, send_sem=send, recv_sem=recv, device_id=to, device_id_type=MESH
        )

    def chip_at(dr, dp):
        return ((yl + dp) % 2) * 4 + (x + dr + 4) % 4

    def nesterov_of(rows):
        new = MOMENTUM_RATE * m_ref[rows, :] + g_ref[rows, :]
        return new, g_ref[rows, :] + MOMENTUM_RATE * new

    own = chip_at(0, 0)

    gx = Gather(lambda dr, dp, h: xs.at[chip_at(dr, dp), pl.ds(h * HALF, HALF)], xp, xm, yp, x_send, x_recv, True)
    cores = []
    for h in range(2):
        rows = pl.ds(h * HALF, HALF)
        new, nest = nesterov_of(rows)
        nm_ref[rows, :] = new
        low = nest.astype(jnp.bfloat16)
        xs[own, rows, :] = low
        mine = pl.ds(pl.multiple_of(c * ROWS + h * HALF, 32), HALF)
        xi[mine, :] = low
        if h == 0:
            pl.semaphore_wait(barrier, len(partners))
        gx.begin(h)
        copy = remote(xi.at[mine], xi.at[mine], xc_send.at[h], xc_recv.at[h], core)
        copy.start()
        cores.append(copy)
    for h in range(2):
        theirs = pl.ds(pl.multiple_of((1 - c) * ROWS + h * HALF, 32), HALF)
        remote(xi.at[theirs], xi.at[theirs], xc_send.at[h], xc_recv.at[h], core).wait_recv()
    for k in range(COLS // 128):
        xt[k * 128 : (k + 1) * 128, :] = xi[:, k * 128 : (k + 1) * 128].T

    def piece_copy(j, src_z, dst_z):
        return remote(
            ps.at[j, dst_z], r1.at[j, src_z], r1_send.at[j, dst_z], r1_recv.at[j, src_z], device(x, yl, c, yh, dst_z)
        )

    def gram(dr, dp, h):
        j = chip_at(dr, dp)
        part = jnp.dot(xs[j, h * HALF : (h + 1) * HALF, :], xt[...], preferred_element_type=jnp.float32)
        ps[j, 2 * h : 2 * h + 2] = part.astype(jnp.bfloat16).reshape(2, PIECE, CHIP)
        for piece in (2 * h, 2 * h + 1):

            @pl.when(piece != z)
            def _(piece=piece):
                piece_copy(j, z, piece).start()

    def pair_copy(xj):
        return remote(s_send.at[xj], s_recv.at[xj], r2_send.at[xj], r2_recv.at[xj], yq)

    def reduce(dr, dp):
        j = chip_at(dr, dp)
        total = ps[j, z].astype(jnp.float32)
        for dz in (1, 3, 2):
            src_z = (z + dz) % 4
            piece_copy(j, src_z, src_z).wait_recv()
            total = total + r1[j, src_z].astype(jnp.float32)
        xj = (x + dr + 4) % 4

        @pl.when((yl + dp) % 2 == yh)
        def _():
            keep[xj] = total

        @pl.when((yl + dp) % 2 != yh)
        def _():
            s_send[xj] = total.astype(jnp.bfloat16)
            pair_copy(xj).start()

    def step(places, h):
        for dr, dp in places:
            gx.arrive(dr, dp, h)
        for dr, dp in places:
            gram(dr, dp, h)

    gram(0, 0, 0)
    gram(0, 0, 1)
    near, far = ((-1, 0), (1, 0), (0, 1)), ((-1, 1), (1, 1), (2, 1))
    step(near, 0)
    reduce(0, 0)
    step(near, 1)
    step(((2, 0),), 0)
    step(((2, 0),), 1)
    for place in near:
        reduce(*place)
    step(far, 0)
    reduce(2, 0)
    step(far, 1)
    for place in far:
        reduce(*place)

    gr = Gather(lambda dr, dp, h: rt.at[chip_at(dr, dp), pl.ds(h * 2, 2)], xp, xm, yp, rt_send, rt_recv, True)

    def col_slot(ref, lane):
        def slot(dr, dp, h):
            first = ((yh + dp) % 2) * 4 + h * 2
            at = (z + dr + 4) % 4
            return ref.at[pl.ds(first, 2), lane, at] if lane is not None else ref.at[pl.ds(first, 2), at]

        return slot

    mine_of, theirs_of = col_slot(ls, c), col_slot(ls, 1 - c)
    gl = Gather(mine_of, zp, zm, yq, l_send, l_recv, False)
    lanes = []

    def to_core(dr, dp, h):
        place = PLACES[(dr, dp)] * 2 + h
        copy = remote(mine_of(dr, dp, h), mine_of(dr, dp, h), lc_send.at[place], lc_recv.at[place], core)
        copy.start()
        lanes.append(copy)

    def from_core(dr, dp, h):
        place = PLACES[(dr, dp)] * 2 + h
        ref = theirs_of(dr, dp, h)
        remote(ref, ref, lc_send.at[place], lc_recv.at[place], core).wait_recv()

    for h in range(2):
        for xj in (2 * h, 2 * h + 1):
            pair_copy(xj).wait_recv()
            total = keep[xj] + s_recv[xj].astype(jnp.float32)
            gf[xj] = total
            low = total.astype(jnp.bfloat16)
            rt[own, xj] = low
            ls[yh * 4 + xj, c, z] = low
        gl.begin(h)
        gr.begin(h)
        to_core(0, 0, h)

    def arrive_l(dr, dp, h):
        gl.arrive(dr, dp, h)
        to_core(dr, dp, h)

    for h in range(2):
        for place in near:
            arrive_l(*place, h)
            gr.arrive(*place, h)
    for h in range(2):
        arrive_l(2, 0, h)
        gr.arrive(2, 0, h)
    for h in range(2):
        for place in far[:2]:
            arrive_l(*place, h)
            gr.arrive(*place, h)
    for h in range(2):
        gr.arrive(2, 1, h)

    def square(j):
        left = rt[j].reshape(ROWS, CHIP)
        right = ls[j].reshape(CHIP, CHIP)
        return jnp.dot(left, right, preferred_element_type=jnp.float32)

    for dr in (0, -1, 1, 2):
        for h in range(2):
            from_core(dr, 0, h)
    total = square(yh * 4)
    for k in range(1, 4):
        total = total + square(yh * 4 + k)
    for h in range(2):
        arrive_l(2, 1, h)
    for dr in (0, -1, 1, 2):
        for h in range(2):
            from_core(dr, 1, h)
    for k in range(4):
        total = total + square((1 - yh) * 4 + k)
    mixing = (COEF_B * gf[...].reshape(ROWS, CHIP) + COEF_C * total).astype(jnp.bfloat16)
    mixing = mixing.reshape(4, PIECE, CHIP)
    for xj in range(4):
        ms[yh * 4 + xj, z] = mixing[xj]
    gm = Gather(col_slot(ms, None), zp, zm, yq, m_send, m_recv, True)
    gm.begin(0)
    gm.begin(1)

    def product(dr, dp, first=False):
        side, at = ((yh + dp) % 2) * 4, (z + dr + 4) % 4
        mt[...] = ms[pl.ds(side, 4), at].reshape(ROWS, CHIP).T
        rows = pl.ds(pl.multiple_of(at * PIECE, 16), PIECE)
        for n in range(3):
            cols = pl.ds(n * 384, 384)
            right = xs[pl.ds(side, 4), rows, cols].reshape(ROWS, 384)
            part = jnp.dot(mt[...], right, preferred_element_type=jnp.float32)
            zs[:, cols] = part if first else zs[:, cols] + part

    product(0, 0, True)
    for h in range(2):
        for place in near:
            gm.arrive(*place, h)
    for h in range(2):
        gm.arrive(2, 0, h)
    for place in near:
        product(*place)
    product(2, 0)
    for place in far:
        for h in range(2):
            gm.arrive(*place, h)
        product(*place)
    theirs = pl.ds(pl.multiple_of((1 - c) * ROWS, 32), ROWS)
    mine = pl.ds(pl.multiple_of(c * ROWS, 32), ROWS)
    last = remote(zs.at[theirs], zr, z_send, z_recv, core)
    last.start()
    last.wait_recv()
    _, nest = nesterov_of(slice(None))
    up_ref[...] = SCALE * (COEF_A * nest + (zs[mine, :] + zr[...]))

    for copy in cores + lanes + [last]:
        copy.wait_send()
    for gather in (gx, gr, gl, gm):
        gather.finish()
    for j in range(8):
        for dz in (1, 2, 3):
            piece_copy(j, z, (z + dz) % 4).wait_send()
    for xj in range(4):
        pair_copy(xj).wait_send()


def local(gradient, momentum):
    shape = jax.ShapeDtypeStruct((ROWS, COLS), jnp.float32)
    vmem = pl.BlockSpec(memory_space=pltpu.VMEM)
    half, full = jnp.bfloat16, jnp.float32
    dma = pltpu.SemaphoreType.DMA
    return pl.pallas_call(
        kernel,
        out_shape=(shape, shape),
        in_specs=[vmem, vmem],
        out_specs=(vmem, vmem),
        scratch_shapes=[
            pltpu.VMEM((8, ROWS, COLS), half),
            pltpu.VMEM((CHIP, COLS), half),
            pltpu.VMEM((COLS, CHIP), half),
            pltpu.VMEM((8, 4, PIECE, CHIP), half),
            pltpu.VMEM((8, 4, PIECE, CHIP), half),
            pltpu.VMEM((4, PIECE, CHIP), full),
            pltpu.VMEM((4, PIECE, CHIP), half),
            pltpu.VMEM((4, PIECE, CHIP), half),
            pltpu.VMEM((4, PIECE, CHIP), full),
            pltpu.VMEM((8, 4, PIECE, CHIP), half),
            pltpu.VMEM((8, 2, 4, PIECE, CHIP), half),
            pltpu.VMEM((8, 4, PIECE, CHIP), half),
            pltpu.VMEM((CHIP, ROWS), half),
            pltpu.VMEM((CHIP, COLS), full),
            pltpu.VMEM((ROWS, COLS), full),
            dma((14,)), dma((16,)), dma((2,)), dma((2,)),
            dma((8, 4)), dma((8, 4)), dma((4,)), dma((4,)),
            dma((14,)), dma((16,)), dma((14,)), dma((16,)),
            dma((16,)), dma((16,)), dma((14,)), dma((16,)),
            dma(()), dma(()),
        ],
        name="muon",
        compiler_params=pltpu.CompilerParams(
            collective_id=0, has_side_effects=True, vmem_limit_bytes=60 * 2**20
        ),
    )(gradient, momentum)


def solution(mesh):
    specs = (P("row", "col"), P("row", "col"))
    return jax.shard_map(local, mesh=mesh, in_specs=specs, out_specs=specs, check_vma=False)
```

time: 378 us -> 141 us (0.37)
  waiting for transfers between devices: 328 us -> 0 us
  Pallas kernels: 0 us -> 137 us
  matrix products: 27.2 us -> 0 us
  between operations: 13.8 us -> 0.65 us
    all_gather x4 -> x0, waiting for transfers between devices: 244 us -> none  [the longest x1 71.9 us: local(): x_slab = lax.all_gather(lowered, 'row', axis=0, tiled=True)]
    pallas_call x0 -> x1, Pallas kernels: none -> 137 us  [local(): pl.pallas_call(kernel, out_shape=(shape, shape), in_specs=[vmem, vmem], o...]
    unnamed x6 -> x0, waiting for transfers between devices: 83.4 us -> none
    dot_general x3 -> x0, matrix products: 27.2 us -> none  [the longest x1 10.9 us: local(): jnp.dot(lax.all_gather(mixing, 'col', axis=1, tiled=True), x_slab, prefer...]
  transfers between devices with their start and end apart: 5 -> 0, of which waited for: 5 -> 0; matrix products, arithmetic and copies ran while one was open for 0% -> 0% of each run, Pallas kernels for 0% -> 0%
where the time goes in v1:
time: 141 us
  Pallas kernels  137 us (97%)
  local copies, waits for them, and re-layouts  3.8 us (3%)
    pallas_call x1, Pallas kernels, local(): pl.pallas_call(kernel, out_shape=(shape, shape), in_specs=[vmem, vmem], o...  137 us
    unnamed x4, local copies, waits for them, and re-layouts  3.8 us

profile of v1, /device:TPU:1, one launch (start us, length us, event | category | flops | bytes accessed | tf_op | source)
XLA Modules:
  0.0 141.0 jit_solution(18436423606503235459)
XLA Ops:
  0.6 136.6 %muon.1 = (f32[320,1152]{1,0:T(8,128)}, f32[320,1152]{1,0:T(8,128)}) custom-call(f32[320,1152]{1,0:T(8,128)} %g_ref.1, f32[320,1152]{1,0:T(8,128)} %m_ref.1), custom_call_target="tpu_custom_call" | custom-call | tf_op jit(solution)/shard_map/muon/pallas_call | solution.py:323
  137.2 0.0 copy-start
  137.2 2.7 %copy.6 = f32[320,1152]{1,0:T(8,128)} copy(f32[320,1152]{1,0:T(8,128)} %get-tuple-element.4) | data formatting | bytes 2949120
  139.9 0.0 copy-done
  139.9 1.1 copy.7
Async XLA Ops:
  137.2 2.7 %copy-start = (f32[320,1152]{1,0:T(8,128)S(1)}, f32[320,1152]{1,0:T(8,128)}, u32[]{:S(2)}) copy-start(f32[320,1152]{1,0:T(8,128)} %get-tuple-element.5) | copy-start | bytes 4423684

commit v2 on v1

--- a/solution.py
+++ b/solution.py
@@ -20,7 +20,13 @@
 HALF = ROWS // 2
 CHIP = 2 * ROWS
 PIECE = ROWS // 4
+MAIN, EXTRA = 32, 16
 PLACES = {(0, 0): 0, (-1, 0): 1, (1, 0): 2, (2, 0): 3, (0, 1): 4, (-1, 1): 5, (1, 1): 6, (2, 1): 7}
+
+
+def spans(h):
+    main = [(MAIN * piece, MAIN, piece, MAIN * h) for piece in range(4)]
+    return main + [(4 * MAIN + EXTRA * e, EXTRA, 2 * h + e, 2 * MAIN) for e in range(2)]
 
 
 class Gather:
@@ -76,9 +82,9 @@
 
 
 def kernel(
-    g_ref, m_ref, nm_ref, up_ref,
-    xs, xi, xt, ps, r1, keep, s_send, s_recv, gf, rt, ls, ms, mt, zs, zr,
-    x_send, x_recv, xc_send, xc_recv, r1_send, r1_recv, r2_send, r2_recv,
+    g_hbm, m_hbm, out_ref,
+    g_ref, m_ref, xs, xi, xt, ps, r1, keep, s_send, s_recv, gf, rt, ls, ms, mt, zs, zr,
+    in_sem, x_send, x_recv, xc_send, xc_recv, r1_send, r1_recv, r2_send, r2_recv,
     rt_send, rt_recv, l_send, l_recv, lc_send, lc_recv, m_send, m_recv, z_send, z_recv,
 ):
     row, col = lax.axis_index("row"), lax.axis_index("col")
@@ -97,6 +103,13 @@
     partners = (core, xp, xm, zp, zm, z2, yp, yq)
     for partner in partners:
         pl.semaphore_signal(barrier, inc=1, device_id=partner, device_id_type=MESH)
+    loads = []
+    for h in range(2):
+        rows = pl.ds(h * HALF, HALF)
+        for k, (hbm, ref) in enumerate(((g_hbm, g_ref), (m_hbm, m_ref))):
+            load = pltpu.make_async_copy(hbm.at[rows], ref.at[rows], in_sem.at[2 * h + k])
+            load.start()
+            loads.append(load)
 
     def remote(src, dst, send, recv, to):
         return pltpu.make_async_remote_copy(
@@ -106,58 +119,62 @@
     def chip_at(dr, dp):
         return ((yl + dp) % 2) * 4 + (x + dr + 4) % 4
 
-    def nesterov_of(rows):
+    own = chip_at(0, 0)
+
+    gx = Gather(lambda dr, dp, h: xs.at[chip_at(dr, dp), pl.ds(h * HALF, HALF)], xp, xm, yp, x_send, x_recv, True)
+    mine = pl.ds(pl.multiple_of(c * ROWS, 32), ROWS)
+    theirs = pl.ds(pl.multiple_of((1 - c) * ROWS, 32), ROWS)
+    for h in range(2):
+        rows = pl.ds(h * HALF, HALF)
+        loads[2 * h].wait()
+        loads[2 * h + 1].wait()
         new = MOMENTUM_RATE * m_ref[rows, :] + g_ref[rows, :]
-        return new, g_ref[rows, :] + MOMENTUM_RATE * new
-
-    own = chip_at(0, 0)
-
-    gx = Gather(lambda dr, dp, h: xs.at[chip_at(dr, dp), pl.ds(h * HALF, HALF)], xp, xm, yp, x_send, x_recv, True)
-    cores = []
-    for h in range(2):
-        rows = pl.ds(h * HALF, HALF)
-        new, nest = nesterov_of(rows)
-        nm_ref[rows, :] = new
-        low = nest.astype(jnp.bfloat16)
+        low = (g_ref[rows, :] + MOMENTUM_RATE * new).astype(jnp.bfloat16)
         xs[own, rows, :] = low
-        mine = pl.ds(pl.multiple_of(c * ROWS + h * HALF, 32), HALF)
-        xi[mine, :] = low
         if h == 0:
             pl.semaphore_wait(barrier, len(partners))
         gx.begin(h)
-        copy = remote(xi.at[mine], xi.at[mine], xc_send.at[h], xc_recv.at[h], core)
-        copy.start()
-        cores.append(copy)
-    for h in range(2):
-        theirs = pl.ds(pl.multiple_of((1 - c) * ROWS + h * HALF, 32), HALF)
-        remote(xi.at[theirs], xi.at[theirs], xc_send.at[h], xc_recv.at[h], core).wait_recv()
+        for first, count, piece, at in spans(h):
+            xi[pl.ds(pl.multiple_of(c * ROWS + piece * PIECE + at, 16), count), :] = low[first : first + count]
+    swap = remote(xi.at[mine], xi.at[mine], xc_send, xc_recv, core)
+    swap.start()
+    remote(xi.at[theirs], xi.at[theirs], xc_send, xc_recv, core).wait_recv()
     for k in range(COLS // 128):
         xt[k * 128 : (k + 1) * 128, :] = xi[:, k * 128 : (k + 1) * 128].T
 
-    def piece_copy(j, src_z, dst_z):
-        return remote(
-            ps.at[j, dst_z], r1.at[j, src_z], r1_send.at[j, dst_z], r1_recv.at[j, src_z], device(x, yl, c, yh, dst_z)
-        )
+    def piece_copy(j, src_z, dst_z, kind):
+        if kind < 2:
+            src = ps.at[j, kind, pl.ds(pl.multiple_of(dst_z * MAIN, MAIN), MAIN)]
+        else:
+            src = ps.at[j, dst_z // 2, pl.ds(pl.multiple_of(4 * MAIN + dst_z % 2 * EXTRA, EXTRA), EXTRA)]
+        dst = r1.at[j, src_z, pl.ds(kind * MAIN, MAIN if kind < 2 else EXTRA)]
+        to = device(x, yl, c, yh, dst_z)
+        return remote(src, dst, r1_send.at[j, dst_z, kind], r1_recv.at[j, src_z, kind], to)
 
     def gram(dr, dp, h):
         j = chip_at(dr, dp)
         part = jnp.dot(xs[j, h * HALF : (h + 1) * HALF, :], xt[...], preferred_element_type=jnp.float32)
-        ps[j, 2 * h : 2 * h + 2] = part.astype(jnp.bfloat16).reshape(2, PIECE, CHIP)
+        ps[j, h] = part.astype(jnp.bfloat16)
+        for dz in (2, 1, 3):
+            piece_copy(j, z, (z + dz) % 4, h).start()
         for piece in (2 * h, 2 * h + 1):
 
             @pl.when(piece != z)
             def _(piece=piece):
-                piece_copy(j, z, piece).start()
+                piece_copy(j, z, piece, 2).start()
 
     def pair_copy(xj):
         return remote(s_send.at[xj], s_recv.at[xj], r2_send.at[xj], r2_recv.at[xj], yq)
 
     def reduce(dr, dp):
         j = chip_at(dr, dp)
-        total = ps[j, z].astype(jnp.float32)
+        own_rows = [ps[j, h, pl.ds(pl.multiple_of(z * MAIN, MAIN), MAIN)] for h in range(2)]
+        own_rows.append(ps[j, z // 2, pl.ds(pl.multiple_of(4 * MAIN + z % 2 * EXTRA, EXTRA), EXTRA)])
+        total = jnp.concatenate(own_rows, axis=0).astype(jnp.float32)
         for dz in (1, 3, 2):
             src_z = (z + dz) % 4
-            piece_copy(j, src_z, src_z).wait_recv()
+            for kind in range(3):
+                piece_copy(j, src_z, src_z, kind).wait_recv()
             total = total + r1[j, src_z].astype(jnp.float32)
         xj = (x + dr + 4) % 4
 
@@ -226,24 +243,27 @@
             rt[own, xj] = low
             ls[yh * 4 + xj, c, z] = low
         gl.begin(h)
+        to_core(0, 0, h)
+    for h in range(2):
         gr.begin(h)
-        to_core(0, 0, h)
 
     def arrive_l(dr, dp, h):
         gl.arrive(dr, dp, h)
         to_core(dr, dp, h)
 
     for h in range(2):
-        for place in near:
-            arrive_l(*place, h)
-            gr.arrive(*place, h)
-    for h in range(2):
+        for arrive in (arrive_l, gr.arrive):
+            arrive(-1, 0, h)
+            arrive(1, 0, h)
+        arrive_l(0, 1, h)
+    for h in range(2):
+        gr.arrive(2, 0, h)
+        gr.arrive(0, 1, h)
         arrive_l(2, 0, h)
-        gr.arrive(2, 0, h)
-    for h in range(2):
-        for place in far[:2]:
-            arrive_l(*place, h)
-            gr.arrive(*place, h)
+    for h in range(2):
+        for arrive in (arrive_l, gr.arrive):
+            arrive(-1, 1, h)
+            arrive(1, 1, h)
     for h in range(2):
         gr.arrive(2, 1, h)
 
@@ -273,63 +293,80 @@
     gm.begin(0)
     gm.begin(1)
 
-    def product(dr, dp, first=False):
+    def rows_of(side, at, cols):
+        blocks = []
+        for k in range(4):
+            for h in range(2):
+                blocks.append(xs[side + k, pl.ds(pl.multiple_of(h * HALF + at * MAIN, MAIN), MAIN), cols])
+            extra = at // 2 * HALF + 4 * MAIN + at % 2 * EXTRA
+            blocks.append(xs[side + k, pl.ds(pl.multiple_of(extra, EXTRA), EXTRA), cols])
+        return jnp.concatenate(blocks, axis=0)
+
+    def turn(dr, dp, slot):
         side, at = ((yh + dp) % 2) * 4, (z + dr + 4) % 4
-        mt[...] = ms[pl.ds(side, 4), at].reshape(ROWS, CHIP).T
-        rows = pl.ds(pl.multiple_of(at * PIECE, 16), PIECE)
+        mt[slot] = ms[pl.ds(side, 4), at].reshape(ROWS, CHIP).T
+
+    def product(dr, dp, slot, rows, first=False):
+        side, at = ((yh + dp) % 2) * 4, (z + dr + 4) % 4
         for n in range(3):
             cols = pl.ds(n * 384, 384)
-            right = xs[pl.ds(side, 4), rows, cols].reshape(ROWS, 384)
-            part = jnp.dot(mt[...], right, preferred_element_type=jnp.float32)
-            zs[:, cols] = part if first else zs[:, cols] + part
-
-    product(0, 0, True)
-    for h in range(2):
-        for place in near:
-            gm.arrive(*place, h)
+            part = jnp.dot(mt[slot, rows, :], rows_of(side, at, cols), preferred_element_type=jnp.float32)
+            zs[rows, cols] = part if first else zs[rows, cols] + part
+
+    every = slice(None)
+    turn(0, 0, 0)
+    product(0, 0, 0, every, True)
+    for h in range(2):
+        gm.arrive(-1, 0, h)
+        gm.arrive(1, 0, h)
+        gm.arrive(0, 1, h)
     for h in range(2):
         gm.arrive(2, 0, h)
-    for place in near:
-        product(*place)
-    product(2, 0)
-    for place in far:
+    for place in near + ((2, 0),):
+        turn(*place, 0)
+        product(*place, 0, every)
+    for k, place in enumerate(far):
         for h in range(2):
             gm.arrive(*place, h)
-        product(*place)
-    theirs = pl.ds(pl.multiple_of((1 - c) * ROWS, 32), ROWS)
-    mine = pl.ds(pl.multiple_of(c * ROWS, 32), ROWS)
+        turn(*place, k)
+        product(*place, k, theirs)
     last = remote(zs.at[theirs], zr, z_send, z_recv, core)
     last.start()
+    for k, place in enumerate(far):
+        product(*place, k, mine)
     last.wait_recv()
-    _, nest = nesterov_of(slice(None))
-    up_ref[...] = SCALE * (COEF_A * nest + (zs[mine, :] + zr[...]))
-
-    for copy in cores + lanes + [last]:
+    total = zs[mine, :] + zr[...]
+    for h in range(2):
+        for first, count, piece, at in spans(h):
+            out_ref[pl.ds(h * HALF + first, count), :] = total[piece * PIECE + at : piece * PIECE + at + count]
+
+    for copy in lanes + [swap, last]:
         copy.wait_send()
     for gather in (gx, gr, gl, gm):
         gather.finish()
     for j in range(8):
         for dz in (1, 2, 3):
-            piece_copy(j, z, (z + dz) % 4).wait_send()
+            for kind in range(3):
+                piece_copy(j, z, (z + dz) % 4, kind).wait_send()
     for xj in range(4):
         pair_copy(xj).wait_send()
 
 
 def local(gradient, momentum):
-    shape = jax.ShapeDtypeStruct((ROWS, COLS), jnp.float32)
-    vmem = pl.BlockSpec(memory_space=pltpu.VMEM)
     half, full = jnp.bfloat16, jnp.float32
     dma = pltpu.SemaphoreType.DMA
-    return pl.pallas_call(
+    product = pl.pallas_call(
         kernel,
-        out_shape=(shape, shape),
-        in_specs=[vmem, vmem],
-        out_specs=(vmem, vmem),
+        out_shape=jax.ShapeDtypeStruct((ROWS, COLS), full),
+        in_specs=[pl.BlockSpec(memory_space=pl.ANY)] * 2,
+        out_specs=pl.BlockSpec(memory_space=pltpu.VMEM),
         scratch_shapes=[
+            pltpu.VMEM((ROWS, COLS), full),
+            pltpu.VMEM((ROWS, COLS), full),
             pltpu.VMEM((8, ROWS, COLS), half),
             pltpu.VMEM((CHIP, COLS), half),
             pltpu.VMEM((COLS, CHIP), half),
-            pltpu.VMEM((8, 4, PIECE, CHIP), half),
+            pltpu.VMEM((8, 2, HALF, CHIP), half),
             pltpu.VMEM((8, 4, PIECE, CHIP), half),
             pltpu.VMEM((4, PIECE, CHIP), full),
             pltpu.VMEM((4, PIECE, CHIP), half),
@@ -338,11 +375,11 @@
             pltpu.VMEM((8, 4, PIECE, CHIP), half),
             pltpu.VMEM((8, 2, 4, PIECE, CHIP), half),
             pltpu.VMEM((8, 4, PIECE, CHIP), half),
-            pltpu.VMEM((CHIP, ROWS), half),
+            pltpu.VMEM((3, CHIP, ROWS), half),
             pltpu.VMEM((CHIP, COLS), full),
             pltpu.VMEM((ROWS, COLS), full),
-            dma((14,)), dma((16,)), dma((2,)), dma((2,)),
-            dma((8, 4)), dma((8, 4)), dma((4,)), dma((4,)),
+            dma((4,)), dma((14,)), dma((16,)), dma(()), dma(()),
+            dma((8, 4, 3)), dma((8, 4, 3)), dma((4,)), dma((4,)),
             dma((14,)), dma((16,)), dma((14,)), dma((16,)),
             dma((16,)), dma((16,)), dma((14,)), dma((16,)),
             dma(()), dma(()),
@@ -352,6 +389,9 @@
             collective_id=0, has_side_effects=True, vmem_limit_bytes=60 * 2**20
         ),
     )(gradient, momentum)
+    new_momentum = MOMENTUM_RATE * momentum + gradient
+    nesterov = gradient + MOMENTUM_RATE * new_momentum
+    return new_momentum, SCALE * (COEF_A * nesterov + product)
 
 
 def solution(mesh):

time: 141 us -> 132 us (0.936)
  Pallas kernels: 137 us -> 128 us
  local copies, waits for them, and re-layouts: 3.8 us -> 0.01 us
  other arithmetic: 0 us -> 3.35 us
    pallas_call x1, Pallas kernels: 137 us -> 128 us  [local(): pl.pallas_call(kernel, out_shape=jax.ShapeDtypeStruct((ROWS, COLS), full)...]
    unnamed x4, local copies, waits for them, and re-layouts: 3.8 us -> 0.01 us
    mul x0 -> x1, other arithmetic: none -> 3.35 us  [local(): return (new_momentum, SCALE * (COEF_A * nesterov + product))]
where the time goes in v2:
time: 132 us
  Pallas kernels  128 us (97%)
  other arithmetic  3.35 us (3%)
    pallas_call x1, Pallas kernels, local(): pl.pallas_call(kernel, out_shape=jax.ShapeDtypeStruct((ROWS, COLS), full)...  128 us
    mul x1, other arithmetic, local(): return (new_momentum, SCALE * (COEF_A * nesterov + product))  3.35 us

profile of v2, /device:TPU:1, one launch (start us, length us, event | category | flops | bytes accessed | tf_op | source)
XLA Modules:
  0.0 132.0 jit_solution(14778339238102777968)
XLA Ops:
  0.6 0.0 copy-start.1
  0.6 0.0 copy-start
  0.6 128.0 %muon.1 = f32[320,1152]{1,0:T(8,128)} custom-call(f32[320,1152]{1,0:T(8,128)} %g_hbm.1, f32[320,1152]{1,0:T(8,128)} %m_hbm.1), custom_call_target="tpu_custom_call" | custom-call | tf_op jit(solution)/shard_map/muon/pallas_call | solution.py:358
  128.6 0.0 copy-done.1
  128.6 0.0 copy-done
  128.7 3.3 %add_multiply_fusion = (f32[320,1152]{1,0:T(8,128)}, f32[320,1152]{1,0:T(8,128)}) fusion(f32[320,1152]{1,0:T(8,128)} %muon.1, f32[320,1152]{1,0:T(8,128)S(1)} %copy-done, f32[320,1152]{1,0:T(8,128)S(1)} %copy-done.1), kind=kLoop, calls=%fused_computation | loop fusion | flops 2580480 | bytes 7372800 | tf_op jit(solution)/shard_map/mul | solution.py:394
Async XLA Ops:
  0.6 128.0 %copy-start.1 = (f32[320,1152]{1,0:T(8,128)S(1)}, f32[320,1152]{1,0:T(8,128)}, u32[]{:S(2)}) copy-start(f32[320,1152]{1,0:T(8,128)} %m_hbm.1) | copy-start | bytes 4423684
  0.6 128.0 %copy-start = (f32[320,1152]{1,0:T(8,128)S(1)}, f32[320,1152]{1,0:T(8,128)}, u32[]{:S(2)}) copy-start(f32[320,1152]{1,0:T(8,128)} %g_hbm.1) | copy-start | bytes 4423684

commit v3 on v2

--- a/solution.py
+++ b/solution.py
@@ -30,9 +30,9 @@
 
 
 class Gather:
-    def __init__(self, slot, plus, minus, pair, send, recv, over_pair):
+    def __init__(self, slot, plus, minus, pair, send, recv, over_pair, hold=False):
         self.slot, self.plus, self.minus, self.pair = slot, plus, minus, pair
-        self.send, self.recv, self.over_pair, self.started = send, recv, over_pair, []
+        self.send, self.recv, self.over_pair, self.hold, self.started = send, recv, over_pair, hold, []
 
     def _copy(self, dr, dp, h, to):
         device, ring, other = {"plus": (self.plus, -1, 0), "minus": (self.minus, 1, 0), "pair": (self.pair, 0, 1)}[to]
@@ -55,6 +55,10 @@
         for to in ("plus", "minus", "pair"):
             self._copy(0, 0, h, to)
 
+    def spread(self, h):
+        self._copy(0, 1, h, "plus")
+        self._copy(0, 1, h, "minus")
+
     def arrive(self, dr, dp, h):
         ref = self.slot(dr, dp, h)
         place = PLACES[(dr, dp)] * 2 + h
@@ -67,8 +71,8 @@
             device_id_type=MESH,
         ).wait_recv()
         if (dr, dp) == (0, 1):
-            self._copy(dr, dp, h, "plus")
-            self._copy(dr, dp, h, "minus")
+            if not self.hold:
+                self.spread(h)
         elif (dr, dp, h) == (-1, 0, 0) or (dr, dp, h, self.over_pair) == (-1, 1, 0, False):
             self._copy(dr, dp, h, "plus")
         elif (dr, dp, h) == (1, 0, 1) or (dr, dp, h, self.over_pair) == (1, 1, 1, False):
@@ -83,8 +87,8 @@
 
 def kernel(
     g_hbm, m_hbm, out_ref,
-    g_ref, m_ref, xs, xi, xt, ps, r1, keep, s_send, s_recv, gf, rt, ls, ms, mt, zs, zr,
-    in_sem, x_send, x_recv, xc_send, xc_recv, r1_send, r1_recv, r2_send, r2_recv,
+    g_ref, m_ref, xs, xi, xq, xt, ps, r1, keep, s_send, s_recv, gf, rt, ls, ms, mt, zs, zr,
+    in_sem, x_send, x_recv, xc_send, xc_recv, xq_send, xq_recv, xq_sem, r1_send, r1_recv, r2_send, r2_recv,
     rt_send, rt_recv, l_send, l_recv, lc_send, lc_recv, m_send, m_recv, z_send, z_recv,
 ):
     row, col = lax.axis_index("row"), lax.axis_index("col")
@@ -99,8 +103,10 @@
     zp, zm = device(x, yl, c, yh, (z + 1) % 4), device(x, yl, c, yh, (z + 3) % 4)
     z2 = device(x, yl, c, yh, (z + 2) % 4)
     yp, yq = device(x, 1 - yl, c, yh, z), device(x, yl, c, 1 - yh, z)
+    yd = device(x, 1 - yl, c, 1 - yh, z)
+    early = yl == yh
     barrier = pltpu.get_barrier_semaphore()
-    partners = (core, xp, xm, zp, zm, z2, yp, yq)
+    partners = (core, xp, xm, zp, zm, z2, yp, yq, yd)
     for partner in partners:
         pl.semaphore_signal(barrier, inc=1, device_id=partner, device_id_type=MESH)
     loads = []
@@ -121,7 +127,7 @@
 
     own = chip_at(0, 0)
 
-    gx = Gather(lambda dr, dp, h: xs.at[chip_at(dr, dp), pl.ds(h * HALF, HALF)], xp, xm, yp, x_send, x_recv, True)
+    gx = Gather(lambda dr, dp, h: xs.at[chip_at(dr, dp), pl.ds(h * HALF, HALF)], xp, xm, yp, x_send, x_recv, False, True)
     mine = pl.ds(pl.multiple_of(c * ROWS, 32), ROWS)
     theirs = pl.ds(pl.multiple_of((1 - c) * ROWS, 32), ROWS)
     for h in range(2):
@@ -140,7 +146,7 @@
     swap.start()
     remote(xi.at[theirs], xi.at[theirs], xc_send, xc_recv, core).wait_recv()
     for k in range(COLS // 128):
-        xt[k * 128 : (k + 1) * 128, :] = xi[:, k * 128 : (k + 1) * 128].T
+        xt[0, k * 128 : (k + 1) * 128, :] = xi[:, k * 128 : (k + 1) * 128].T
 
     def piece_copy(j, src_z, dst_z, kind):
         if kind < 2:
@@ -151,62 +157,105 @@
         to = device(x, yl, c, yh, dst_z)
         return remote(src, dst, r1_send.at[j, dst_z, kind], r1_recv.at[j, src_z, kind], to)
 
-    def gram(dr, dp, h):
-        j = chip_at(dr, dp)
-        part = jnp.dot(xs[j, h * HALF : (h + 1) * HALF, :], xt[...], preferred_element_type=jnp.float32)
-        ps[j, h] = part.astype(jnp.bfloat16)
+    def block_of(i, dr):
+        return i * 4 + (x + dr + 4) % 4
+
+    def gram(i, dr, h):
+        j, block = chip_at(dr, 0), block_of(i, dr)
+        part = jnp.dot(xs[j, h * HALF : (h + 1) * HALF, :], xt[i], preferred_element_type=jnp.float32)
+        ps[block, h] = part.astype(jnp.bfloat16)
         for dz in (2, 1, 3):
-            piece_copy(j, z, (z + dz) % 4, h).start()
+            piece_copy(block, z, (z + dz) % 4, h).start()
         for piece in (2 * h, 2 * h + 1):
 
             @pl.when(piece != z)
             def _(piece=piece):
-                piece_copy(j, z, piece, 2).start()
-
-    def pair_copy(xj):
-        return remote(s_send.at[xj], s_recv.at[xj], r2_send.at[xj], r2_recv.at[xj], yq)
-
-    def reduce(dr, dp):
-        j = chip_at(dr, dp)
-        own_rows = [ps[j, h, pl.ds(pl.multiple_of(z * MAIN, MAIN), MAIN)] for h in range(2)]
-        own_rows.append(ps[j, z // 2, pl.ds(pl.multiple_of(4 * MAIN + z % 2 * EXTRA, EXTRA), EXTRA)])
+                piece_copy(block, z, piece, 2).start()
+
+    def sum_copy(i, xj, slot, to):
+        return remote(s_send.at[i, xj], s_recv.at[slot, xj], r2_send.at[i, xj], r2_recv.at[slot, xj], to)
+
+    def sum_arrive(slot, xj):
+        ref = s_recv.at[slot, xj]
+        remote(ref, ref, r2_send.at[0, xj], r2_recv.at[slot, xj], yp).wait_recv()
+
+    def reduce(i, dr):
+        block = block_of(i, dr)
+        own_rows = [ps[block, h, pl.ds(pl.multiple_of(z * MAIN, MAIN), MAIN)] for h in range(2)]
+        own_rows.append(ps[block, z // 2, pl.ds(pl.multiple_of(4 * MAIN + z % 2 * EXTRA, EXTRA), EXTRA)])
         total = jnp.concatenate(own_rows, axis=0).astype(jnp.float32)
         for dz in (1, 3, 2):
             src_z = (z + dz) % 4
             for kind in range(3):
-                piece_copy(j, src_z, src_z, kind).wait_recv()
-            total = total + r1[j, src_z].astype(jnp.float32)
+                piece_copy(block, src_z, src_z, kind).wait_recv()
+            total = total + r1[block, src_z].astype(jnp.float32)
         xj = (x + dr + 4) % 4
-
-        @pl.when((yl + dp) % 2 == yh)
-        def _():
-            keep[xj] = total
-
-        @pl.when((yl + dp) % 2 != yh)
-        def _():
-            s_send[xj] = total.astype(jnp.bfloat16)
-            pair_copy(xj).start()
-
-    def step(places, h):
-        for dr, dp in places:
-            gx.arrive(dr, dp, h)
-        for dr, dp in places:
-            gram(dr, dp, h)
+        if i == 0:
+
+            @pl.when(early)
+            def _():
+                keep[xj] = total
+
+            @pl.when(jnp.logical_not(early))
+            def _():
+                s_send[i, xj] = total.astype(jnp.bfloat16)
+                sum_copy(i, xj, 0, yq).start()
+
+        else:
+            s_send[i, xj] = total.astype(jnp.bfloat16)
+
+            @pl.when(early)
+            def _():
+                sum_copy(i, xj, 0, yp).start()
+
+            @pl.when(jnp.logical_not(early))
+            def _():
+                sum_copy(i, xj, 1, yd).start()
+
+    def pass_pair(h):
+        rows = pl.ds(h * HALF, HALF)
+        src = xs.at[chip_at(0, 1), rows]
+        over = remote(src, xq.at[c, rows], xq_send.at[h], xq_recv.at[h], core)
+        over.start()
+        here = pltpu.make_async_copy(src, xq.at[c, rows], xq_sem.at[h])
+        here.start()
+        return over, here
 
     gram(0, 0, 0)
     gram(0, 0, 1)
-    near, far = ((-1, 0), (1, 0), (0, 1)), ((-1, 1), (1, 1), (2, 1))
-    step(near, 0)
+    passed = []
+    for h in range(2):
+        gx.arrive(-1, 0, h)
+        gx.arrive(1, 0, h)
+        gx.arrive(0, 1, h)
+        passed.append(pass_pair(h))
+        gram(0, -1, h)
+        gram(0, 1, h)
+    for h in range(2):
+        gx.spread(h)
+    for h in range(2):
+        ref = xq.at[1 - c, pl.ds(h * HALF, HALF)]
+        remote(ref, ref, xq_send.at[h], xq_recv.at[h], core).wait_recv()
+        passed[h][1].wait()
+    for k in range(COLS // 128):
+        cols = slice(k * 128, (k + 1) * 128)
+        blocks = []
+        for lane in range(2):
+            for piece in range(4):
+                for first in (MAIN * piece, HALF + MAIN * piece):
+                    blocks.append(xq[lane, first : first + MAIN, cols])
+                first = piece // 2 * HALF + 4 * MAIN + piece % 2 * EXTRA
+                blocks.append(xq[lane, first : first + EXTRA, cols])
+        xt[1, cols, :] = jnp.concatenate(blocks, axis=0).T
+    for dr in (0, -1, 1):
+        for h in range(2):
+            gram(1, dr, h)
     reduce(0, 0)
-    step(near, 1)
-    step(((2, 0),), 0)
-    step(((2, 0),), 1)
-    for place in near:
-        reduce(*place)
-    step(far, 0)
-    reduce(2, 0)
-    step(far, 1)
-    for place in far:
+    for h in range(2):
+        gx.arrive(2, 0, h)
+        for i in range(2):
+            gram(i, 2, h)
+    for place in ((0, -1), (0, 1), (1, 0), (1, -1), (1, 1), (0, 2), (1, 2)):
         reduce(*place)
 
     gr = Gather(lambda dr, dp, h: rt.at[chip_at(dr, dp), pl.ds(h * 2, 2)], xp, xm, yp, rt_send, rt_recv, True)
@@ -236,8 +285,14 @@
 
     for h in range(2):
         for xj in (2 * h, 2 * h + 1):
-            pair_copy(xj).wait_recv()
-            total = keep[xj] + s_recv[xj].astype(jnp.float32)
+            sum_arrive(0, xj)
+
+            @pl.when(jnp.logical_not(early))
+            def _(xj=xj):
+                sum_arrive(1, xj)
+                keep[xj] = s_recv[1, xj].astype(jnp.float32)
+
+            total = keep[xj] + s_recv[0, xj].astype(jnp.float32)
             gf[xj] = total
             low = total.astype(jnp.bfloat16)
             rt[own, xj] = low
@@ -247,6 +302,8 @@
     for h in range(2):
         gr.begin(h)
 
+    near, far = ((-1, 0), (1, 0), (0, 1)), ((-1, 1), (1, 1), (2, 1))
+
     def arrive_l(dr, dp, h):
         gl.arrive(dr, dp, h)
         to_core(dr, dp, h)
@@ -266,6 +323,8 @@
             arrive(1, 1, h)
     for h in range(2):
         gr.arrive(2, 1, h)
+        gx.arrive(-1, 1, h)
+        gx.arrive(1, 1, h)
 
     def square(j):
         left = rt[j].reshape(ROWS, CHIP)
@@ -314,6 +373,8 @@
             zs[rows, cols] = part if first else zs[rows, cols] + part
 
     every = slice(None)
+    for h in range(2):
+        gx.arrive(2, 1, h)
     turn(0, 0, 0)
     product(0, 0, 0, every, True)
     for h in range(2):
@@ -340,7 +401,7 @@
         for first, count, piece, at in spans(h):
             out_ref[pl.ds(h * HALF + first, count), :] = total[piece * PIECE + at : piece * PIECE + at + count]
 
-    for copy in lanes + [swap, last]:
+    for copy in lanes + [swap, last] + [over for over, _ in passed]:
         copy.wait_send()
     for gather in (gx, gr, gl, gm):
         gather.finish()
@@ -349,7 +410,11 @@
             for kind in range(3):
                 piece_copy(j, z, (z + dz) % 4, kind).wait_send()
     for xj in range(4):
-        pair_copy(xj).wait_send()
+        sum_copy(1, xj, 0, yp).wait_send()
+
+        @pl.when(jnp.logical_not(early))
+        def _(xj=xj):
+            sum_copy(0, xj, 0, yq).wait_send()
 
 
 def local(gradient, momentum):
@@ -365,12 +430,13 @@
             pltpu.VMEM((ROWS, COLS), full),
             pltpu.VMEM((8, ROWS, COLS), half),
             pltpu.VMEM((CHIP, COLS), half),
-            pltpu.VMEM((COLS, CHIP), half),
+            pltpu.VMEM((2, ROWS, COLS), half),
+            pltpu.VMEM((2, COLS, CHIP), half),
             pltpu.VMEM((8, 2, HALF, CHIP), half),
             pltpu.VMEM((8, 4, PIECE, CHIP), half),
             pltpu.VMEM((4, PIECE, CHIP), full),
-            pltpu.VMEM((4, PIECE, CHIP), half),
-            pltpu.VMEM((4, PIECE, CHIP), half),
+            pltpu.VMEM((2, 4, PIECE, CHIP), half),
+            pltpu.VMEM((2, 4, PIECE, CHIP), half),
             pltpu.VMEM((4, PIECE, CHIP), full),
             pltpu.VMEM((8, 4, PIECE, CHIP), half),
             pltpu.VMEM((8, 2, 4, PIECE, CHIP), half),
@@ -378,8 +444,8 @@
             pltpu.VMEM((3, CHIP, ROWS), half),
             pltpu.VMEM((CHIP, COLS), full),
             pltpu.VMEM((ROWS, COLS), full),
-            dma((4,)), dma((14,)), dma((16,)), dma(()), dma(()),
-            dma((8, 4, 3)), dma((8, 4, 3)), dma((4,)), dma((4,)),
+            dma((4,)), dma((14,)), dma((16,)), dma(()), dma(()), dma((2,)), dma((2,)), dma((2,)),
+            dma((8, 4, 3)), dma((8, 4, 3)), dma((2, 4)), dma((2, 4)),
             dma((14,)), dma((16,)), dma((14,)), dma((16,)),
             dma((16,)), dma((16,)), dma((14,)), dma((16,)),
             dma(()), dma(()),

time: 132 us -> 133 us (level)
  no operation moved by 1% of the time
where the time goes in v3:
time: 133 us
  Pallas kernels  129 us (97%)
  other arithmetic  3.35 us (3%)
    pallas_call x1, Pallas kernels, local(): pl.pallas_call(kernel, out_shape=jax.ShapeDtypeStruct((ROWS, COLS), full)...  129 us
    mul x1, other arithmetic, local(): return (new_momentum, SCALE * (COEF_A * nesterov + product))  3.35 us

profile of v3, /device:TPU:1, one launch (start us, length us, event | category | flops | bytes accessed | tf_op | source)
XLA Modules:
  0.0 132.7 jit_solution(1392739029435880343)
XLA Ops:
  0.6 0.0 copy-start.1
  0.6 0.0 copy-start
  0.6 128.7 %muon.1 = f32[320,1152]{1,0:T(8,128)} custom-call(f32[320,1152]{1,0:T(8,128)} %g_hbm.1, f32[320,1152]{1,0:T(8,128)} %m_hbm.1), custom_call_target="tpu_custom_call" | custom-call | tf_op jit(solution)/shard_map/muon/pallas_call | solution.py:423
  129.3 0.0 copy-done.1
  129.3 0.0 copy-done
  129.3 3.3 %add_multiply_fusion = (f32[320,1152]{1,0:T(8,128)}, f32[320,1152]{1,0:T(8,128)}) fusion(f32[320,1152]{1,0:T(8,128)} %muon.1, f32[320,1152]{1,0:T(8,128)S(1)} %copy-done, f32[320,1152]{1,0:T(8,128)S(1)} %copy-done.1), kind=kLoop, calls=%fused_computation | loop fusion | flops 2580480 | bytes 7372800 | tf_op jit(solution)/shard_map/mul | solution.py:460
Async XLA Ops:
  0.6 128.7 %copy-start.1 = (f32[320,1152]{1,0:T(8,128)S(1)}, f32[320,1152]{1,0:T(8,128)}, u32[]{:S(2)}) copy-start(f32[320,1152]{1,0:T(8,128)} %m_hbm.1) | copy-start | bytes 4423684
  0.6 128.7 %copy-start = (f32[320,1152]{1,0:T(8,128)S(1)}, f32[320,1152]{1,0:T(8,128)}, u32[]{:S(2)}) copy-start(f32[320,1152]{1,0:T(8,128)} %g_hbm.1) | copy-start | bytes 4423684

commit v4 on v3

--- a/solution.py
+++ b/solution.py
@@ -21,6 +21,7 @@
 CHIP = 2 * ROWS
 PIECE = ROWS // 4
 MAIN, EXTRA = 32, 16
+ORDER = (0, -1, 1, 2)
 PLACES = {(0, 0): 0, (-1, 0): 1, (1, 0): 2, (2, 0): 3, (0, 1): 4, (-1, 1): 5, (1, 1): 6, (2, 1): 7}
 
 
@@ -30,15 +31,16 @@
 
 
 class Gather:
-    def __init__(self, slot, plus, minus, pair, send, recv, over_pair, hold=False):
+    def __init__(self, slot, plus, minus, pair, send, recv, over_pair, parts=2, hold=False):
         self.slot, self.plus, self.minus, self.pair = slot, plus, minus, pair
-        self.send, self.recv, self.over_pair, self.hold, self.started = send, recv, over_pair, hold, []
+        self.send, self.recv, self.over_pair = send, recv, over_pair
+        self.parts, self.hold, self.started = parts, hold, []
 
     def _copy(self, dr, dp, h, to):
         device, ring, other = {"plus": (self.plus, -1, 0), "minus": (self.minus, 1, 0), "pair": (self.pair, 0, 1)}[to]
         there = dr + ring
         there = 2 if there == -2 else there
-        place = PLACES[(there, (dp + other) % 2)] * 2 + h
+        place = PLACES[(there, (dp + other) % 2)] * self.parts + h
         ref = self.slot(dr, dp, h)
         copy = pltpu.make_async_remote_copy(
             src_ref=ref,
@@ -61,7 +63,7 @@
 
     def arrive(self, dr, dp, h):
         ref = self.slot(dr, dp, h)
-        place = PLACES[(dr, dp)] * 2 + h
+        place = PLACES[(dr, dp)] * self.parts + h
         pltpu.make_async_remote_copy(
             src_ref=ref,
             dst_ref=ref,
@@ -73,9 +75,9 @@
         if (dr, dp) == (0, 1):
             if not self.hold:
                 self.spread(h)
-        elif (dr, dp, h) == (-1, 0, 0) or (dr, dp, h, self.over_pair) == (-1, 1, 0, False):
+        elif dr == -1 and h % 2 == 0 and not (dp and self.over_pair):
             self._copy(dr, dp, h, "plus")
-        elif (dr, dp, h) == (1, 0, 1) or (dr, dp, h, self.over_pair) == (1, 1, 1, False):
+        elif dr == 1 and h % 2 == 1 and not (dp and self.over_pair):
             self._copy(dr, dp, h, "minus")
         elif (dr, dp) == (2, 0) and self.over_pair:
             self._copy(dr, dp, h, "pair")
@@ -127,7 +129,7 @@
 
     own = chip_at(0, 0)
 
-    gx = Gather(lambda dr, dp, h: xs.at[chip_at(dr, dp), pl.ds(h * HALF, HALF)], xp, xm, yp, x_send, x_recv, False, True)
+    gx = Gather(lambda dr, dp, h: xs.at[chip_at(dr, dp), pl.ds(h * HALF, HALF)], xp, xm, yp, x_send, x_recv, False, hold=True)
     mine = pl.ds(pl.multiple_of(c * ROWS, 32), ROWS)
     theirs = pl.ds(pl.multiple_of((1 - c) * ROWS, 32), ROWS)
     for h in range(2):
@@ -221,6 +223,68 @@
         here.start()
         return over, here
 
+    def row_slot(dr, dp, k):
+        return rt.at[chip_at(dr, dp), (x + dr + ORDER[k] + 4) % 4]
+
+    def col_slot(lane):
+        def slot(dr, dp, k):
+            return ls.at[((yh + dp) % 2) * 4 + (x + ORDER[k] + 4) % 4, lane, (z + dr + 4) % 4]
+
+        return slot
+
+    gr = Gather(row_slot, xp, xm, yp, rt_send, rt_recv, True, 4)
+    mine_of, theirs_of = col_slot(c), col_slot(1 - c)
+    gl = Gather(mine_of, zp, zm, yq, l_send, l_recv, False, 4)
+    lanes = []
+
+    def to_core(dr, dp, k):
+        place = PLACES[(dr, dp)] * 4 + k
+        copy = remote(mine_of(dr, dp, k), mine_of(dr, dp, k), lc_send.at[place], lc_recv.at[place], core)
+        copy.start()
+        lanes.append(copy)
+
+    def from_core(dr, dp, k):
+        place = PLACES[(dr, dp)] * 4 + k
+        ref = theirs_of(dr, dp, k)
+        remote(ref, ref, lc_send.at[place], lc_recv.at[place], core).wait_recv()
+
+    def arrive_l(dr, dp, k):
+        gl.arrive(dr, dp, k)
+        to_core(dr, dp, k)
+
+    def finish_sum(k):
+        xj = (x + ORDER[k] + 4) % 4
+        sum_arrive(0, xj)
+
+        @pl.when(jnp.logical_not(early))
+        def _():
+            sum_arrive(1, xj)
+            keep[xj] = s_recv[1, xj].astype(jnp.float32)
+
+        total = keep[xj] + s_recv[0, xj].astype(jnp.float32)
+        gf[xj] = total
+        low = total.astype(jnp.bfloat16)
+        ls[yh * 4 + xj, c, z] = low
+        gl.begin(k)
+        rt[own, xj] = low
+        gr.begin(k)
+        to_core(0, 0, k)
+
+    def near_of(k):
+        for arrive in (arrive_l, gr.arrive):
+            arrive(-1, 0, k)
+            arrive(1, 0, k)
+        arrive_l(0, 1, k)
+        gr.arrive(0, 1, k)
+
+    def far_of(k):
+        gr.arrive(2, 0, k)
+        for arrive in (arrive_l, gr.arrive):
+            arrive(-1, 1, k)
+            arrive(1, 1, k)
+        arrive_l(2, 0, k)
+
+    near, far = ((-1, 0), (1, 0), (0, 1)), ((-1, 1), (1, 1), (2, 1))
     gram(0, 0, 0)
     gram(0, 0, 1)
     passed = []
@@ -231,6 +295,8 @@
         passed.append(pass_pair(h))
         gram(0, -1, h)
         gram(0, 1, h)
+        if h == 0:
+            reduce(0, 0)
     for h in range(2):
         gx.spread(h)
     for h in range(2):
@@ -250,79 +316,32 @@
     for dr in (0, -1, 1):
         for h in range(2):
             gram(1, dr, h)
-    reduce(0, 0)
     for h in range(2):
         gx.arrive(2, 0, h)
         for i in range(2):
             gram(i, 2, h)
-    for place in ((0, -1), (0, 1), (1, 0), (1, -1), (1, 1), (0, 2), (1, 2)):
-        reduce(*place)
-
-    gr = Gather(lambda dr, dp, h: rt.at[chip_at(dr, dp), pl.ds(h * 2, 2)], xp, xm, yp, rt_send, rt_recv, True)
-
-    def col_slot(ref, lane):
-        def slot(dr, dp, h):
-            first = ((yh + dp) % 2) * 4 + h * 2
-            at = (z + dr + 4) % 4
-            return ref.at[pl.ds(first, 2), lane, at] if lane is not None else ref.at[pl.ds(first, 2), at]
-
-        return slot
-
-    mine_of, theirs_of = col_slot(ls, c), col_slot(ls, 1 - c)
-    gl = Gather(mine_of, zp, zm, yq, l_send, l_recv, False)
-    lanes = []
-
-    def to_core(dr, dp, h):
-        place = PLACES[(dr, dp)] * 2 + h
-        copy = remote(mine_of(dr, dp, h), mine_of(dr, dp, h), lc_send.at[place], lc_recv.at[place], core)
-        copy.start()
-        lanes.append(copy)
-
-    def from_core(dr, dp, h):
-        place = PLACES[(dr, dp)] * 2 + h
-        ref = theirs_of(dr, dp, h)
-        remote(ref, ref, lc_send.at[place], lc_recv.at[place], core).wait_recv()
-
-    for h in range(2):
-        for xj in (2 * h, 2 * h + 1):
-            sum_arrive(0, xj)
-
-            @pl.when(jnp.logical_not(early))
-            def _(xj=xj):
-                sum_arrive(1, xj)
-                keep[xj] = s_recv[1, xj].astype(jnp.float32)
-
-            total = keep[xj] + s_recv[0, xj].astype(jnp.float32)
-            gf[xj] = total
-            low = total.astype(jnp.bfloat16)
-            rt[own, xj] = low
-            ls[yh * 4 + xj, c, z] = low
-        gl.begin(h)
-        to_core(0, 0, h)
-    for h in range(2):
-        gr.begin(h)
-
-    near, far = ((-1, 0), (1, 0), (0, 1)), ((-1, 1), (1, 1), (2, 1))
-
-    def arrive_l(dr, dp, h):
-        gl.arrive(dr, dp, h)
-        to_core(dr, dp, h)
-
-    for h in range(2):
-        for arrive in (arrive_l, gr.arrive):
-            arrive(-1, 0, h)
-            arrive(1, 0, h)
-        arrive_l(0, 1, h)
-    for h in range(2):
-        gr.arrive(2, 0, h)
-        gr.arrive(0, 1, h)
-        arrive_l(2, 0, h)
-    for h in range(2):
-        for arrive in (arrive_l, gr.arrive):
-            arrive(-1, 1, h)
-            arrive(1, 1, h)
-    for h in range(2):
-        gr.arrive(2, 1, h)
+    reduce(0, -1)
+    reduce(0, 1)
+    reduce(1, 0)
+    finish_sum(0)
+    reduce(1, -1)
+    finish_sum(1)
+    reduce(1, 1)
+    finish_sum(2)
+    near_of(0)
+    reduce(0, 2)
+    reduce(1, 2)
+    finish_sum(3)
+    near_of(1)
+    far_of(0)
+    near_of(2)
+    far_of(1)
+    near_of(3)
+    far_of(2)
+    far_of(3)
+    for k in range(4):
+        gr.arrive(2, 1, k)
+    for h in range(2):
         gx.arrive(-1, 1, h)
         gx.arrive(1, 1, h)
 
@@ -332,23 +351,26 @@
         return jnp.dot(left, right, preferred_element_type=jnp.float32)
 
     for dr in (0, -1, 1, 2):
-        for h in range(2):
-            from_core(dr, 0, h)
+        for k in range(4):
+            from_core(dr, 0, k)
     total = square(yh * 4)
     for k in range(1, 4):
         total = total + square(yh * 4 + k)
-    for h in range(2):
-        arrive_l(2, 1, h)
+    for k in range(4):
+        arrive_l(2, 1, k)
     for dr in (0, -1, 1, 2):
-        for h in range(2):
-            from_core(dr, 1, h)
+        for k in range(4):
+            from_core(dr, 1, k)
     for k in range(4):
         total = total + square((1 - yh) * 4 + k)
     mixing = (COEF_B * gf[...].reshape(ROWS, CHIP) + COEF_C * total).astype(jnp.bfloat16)
     mixing = mixing.reshape(4, PIECE, CHIP)
     for xj in range(4):
         ms[yh * 4 + xj, z] = mixing[xj]
-    gm = Gather(col_slot(ms, None), zp, zm, yq, m_send, m_recv, True)
+    def mix_slot(dr, dp, h):
+        return ms.at[pl.ds(((yh + dp) % 2) * 4 + h * 2, 2), (z + dr + 4) % 4]
+
+    gm = Gather(mix_slot, zp, zm, yq, m_send, m_recv, True)
     gm.begin(0)
     gm.begin(1)
 
@@ -446,8 +468,8 @@
             pltpu.VMEM((ROWS, COLS), full),
             dma((4,)), dma((14,)), dma((16,)), dma(()), dma(()), dma((2,)), dma((2,)), dma((2,)),
             dma((8, 4, 3)), dma((8, 4, 3)), dma((2, 4)), dma((2, 4)),
-            dma((14,)), dma((16,)), dma((14,)), dma((16,)),
-            dma((16,)), dma((16,)), dma((14,)), dma((16,)),
+            dma((28,)), dma((32,)), dma((28,)), dma((32,)),
+            dma((32,)), dma((32,)), dma((14,)), dma((16,)),
             dma(()), dma(()),
         ],
         name="muon",

time: 133 us -> 127 us (0.955)
  Pallas kernels: 129 us -> 123 us
    pallas_call x1, Pallas kernels: 129 us -> 123 us  [local(): pl.pallas_call(kernel, out_shape=jax.ShapeDtypeStruct((ROWS, COLS), full)...]
where the time goes in v4:
time: 127 us
  Pallas kernels  123 us (97%)
  other arithmetic  3.35 us (3%)
    pallas_call x1, Pallas kernels, local(): pl.pallas_call(kernel, out_shape=jax.ShapeDtypeStruct((ROWS, COLS), full)...  123 us
    mul x1, other arithmetic, local(): return (new_momentum, SCALE * (COEF_A * nesterov + product))  3.35 us

profile of v4, /device:TPU:1, one launch (start us, length us, event | category | flops | bytes accessed | tf_op | source)
XLA Modules:
  0.0 126.9 jit_solution(11097584683252093594)
XLA Ops:
  0.6 0.0 copy-start.1
  0.6 0.0 copy-start
  0.6 122.9 %muon.1 = f32[320,1152]{1,0:T(8,128)} custom-call(f32[320,1152]{1,0:T(8,128)} %g_hbm.1, f32[320,1152]{1,0:T(8,128)} %m_hbm.1), custom_call_target="tpu_custom_call" | custom-call | tf_op jit(solution)/shard_map/muon/pallas_call | solution.py:445
  123.5 0.0 copy-done.1
  123.6 0.0 copy-done
  123.6 3.3 %add_multiply_fusion = (f32[320,1152]{1,0:T(8,128)}, f32[320,1152]{1,0:T(8,128)}) fusion(f32[320,1152]{1,0:T(8,128)} %muon.1, f32[320,1152]{1,0:T(8,128)S(1)} %copy-done, f32[320,1152]{1,0:T(8,128)S(1)} %copy-done.1), kind=kLoop, calls=%fused_computation | loop fusion | flops 2580480 | bytes 7372800 | tf_op jit(solution)/shard_map/mul | solution.py:482
Async XLA Ops:
  0.6 122.9 %copy-start.1 = (f32[320,1152]{1,0:T(8,128)S(1)}, f32[320,1152]{1,0:T(8,128)}, u32[]{:S(2)}) copy-start(f32[320,1152]{1,0:T(8,128)} %m_hbm.1) | copy-start | bytes 4423684
  0.6 122.9 %copy-start = (f32[320,1152]{1,0:T(8,128)S(1)}, f32[320,1152]{1,0:T(8,128)}, u32[]{:S(2)}) copy-start(f32[320,1152]{1,0:T(8,128)} %g_hbm.1) | copy-start | bytes 4423684

commit v5 on v4

--- a/solution.py
+++ b/solution.py
@@ -20,20 +20,14 @@
 HALF = ROWS // 2
 CHIP = 2 * ROWS
 PIECE = ROWS // 4
-MAIN, EXTRA = 32, 16
 ORDER = (0, -1, 1, 2)
 PLACES = {(0, 0): 0, (-1, 0): 1, (1, 0): 2, (2, 0): 3, (0, 1): 4, (-1, 1): 5, (1, 1): 6, (2, 1): 7}
 
 
-def spans(h):
-    main = [(MAIN * piece, MAIN, piece, MAIN * h) for piece in range(4)]
-    return main + [(4 * MAIN + EXTRA * e, EXTRA, 2 * h + e, 2 * MAIN) for e in range(2)]
-
-
 class Gather:
-    def __init__(self, slot, plus, minus, pair, send, recv, over_pair, parts=2, hold=False):
+    def __init__(self, slot, plus, minus, pair, send, recv, cross, parts=2, hold=False):
         self.slot, self.plus, self.minus, self.pair = slot, plus, minus, pair
-        self.send, self.recv, self.over_pair = send, recv, over_pair
+        self.send, self.recv, self.cross = send, recv, cross
         self.parts, self.hold, self.started = parts, hold, []
 
     def _copy(self, dr, dp, h, to):
@@ -53,13 +47,15 @@
         copy.start()
         self.started.append(copy)
 
-    def begin(self, h):
-        for to in ("plus", "minus", "pair"):
+    def begin(self, h, links=("plus", "minus", "pair")):
+        for to in links:
             self._copy(0, 0, h, to)
 
     def spread(self, h):
-        self._copy(0, 1, h, "plus")
-        self._copy(0, 1, h, "minus")
+        if not self.cross or h % 2 == 1:
+            self._copy(0, 1, h, "plus")
+        if not self.cross or h % 2 == 0:
+            self._copy(0, 1, h, "minus")
 
     def arrive(self, dr, dp, h):
         ref = self.slot(dr, dp, h)
@@ -75,12 +71,10 @@
         if (dr, dp) == (0, 1):
             if not self.hold:
                 self.spread(h)
-        elif dr == -1 and h % 2 == 0 and not (dp and self.over_pair):
-            self._copy(dr, dp, h, "plus")
-        elif dr == 1 and h % 2 == 1 and not (dp and self.over_pair):
-            self._copy(dr, dp, h, "minus")
-        elif (dr, dp) == (2, 0) and self.over_pair:
-            self._copy(dr, dp, h, "pair")
+        elif (dr, h % 2) in ((-1, 0), (1, 1)):
+            self._copy(dr, dp, h, "plus" if dr == -1 else "minus")
+            if self.cross and dp == 0:
+                self._copy(dr, dp, h, "pair")
 
     def finish(self):
         for copy in self.started:
@@ -89,8 +83,8 @@
 
 def kernel(
     g_hbm, m_hbm, out_ref,
-    g_ref, m_ref, xs, xi, xq, xt, ps, r1, keep, s_send, s_recv, gf, rt, ls, ms, mt, zs, zr,
-    in_sem, x_send, x_recv, xc_send, xc_recv, xq_send, xq_recv, xq_sem, r1_send, r1_recv, r2_send, r2_recv,
+    g_ref, m_ref, xs, xi, xq, xt, ps, rl, mg, r1, keep, s_send, s_recv, gf, sq, rt, ls, ms, mt, zs, zb, zr,
+    in_sem, x_send, x_recv, xc_send, xc_recv, xq_send, xq_recv, xq_sem, rl_send, rl_recv, r1_send, r1_recv, r2_send, r2_recv,
     rt_send, rt_recv, l_send, l_recv, lc_send, lc_recv, m_send, m_recv, z_send, z_recv,
 ):
     row, col = lax.axis_index("row"), lax.axis_index("col")
@@ -103,12 +97,11 @@
     core = device(x, yl, 1 - c, yh, z)
     xp, xm = device((x + 1) % 4, yl, c, yh, z), device((x + 3) % 4, yl, c, yh, z)
     zp, zm = device(x, yl, c, yh, (z + 1) % 4), device(x, yl, c, yh, (z + 3) % 4)
-    z2 = device(x, yl, c, yh, (z + 2) % 4)
     yp, yq = device(x, 1 - yl, c, yh, z), device(x, yl, c, 1 - yh, z)
     yd = device(x, 1 - yl, c, 1 - yh, z)
     early = yl == yh
     barrier = pltpu.get_barrier_semaphore()
-    partners = (core, xp, xm, zp, zm, z2, yp, yq, yd)
+    partners = (core, xp, xm, zp, zm, yp, yq, yd)
     for partner in partners:
         pl.semaphore_signal(barrier, inc=1, device_id=partner, device_id_type=MESH)
     loads = []
@@ -141,38 +134,53 @@
         xs[own, rows, :] = low
         if h == 0:
             pl.semaphore_wait(barrier, len(partners))
-        gx.begin(h)
-        for first, count, piece, at in spans(h):
-            xi[pl.ds(pl.multiple_of(c * ROWS + piece * PIECE + at, 16), count), :] = low[first : first + count]
+            gx.begin(0, ("plus", "pair"))
+        else:
+            gx.begin(1, ("minus", "plus", "pair"))
+            gx.begin(0, ("minus",))
+        xi[pl.ds(pl.multiple_of(c * ROWS + h * HALF, 32), HALF), :] = low
     swap = remote(xi.at[mine], xi.at[mine], xc_send, xc_recv, core)
     swap.start()
     remote(xi.at[theirs], xi.at[theirs], xc_send, xc_recv, core).wait_recv()
     for k in range(COLS // 128):
         xt[0, k * 128 : (k + 1) * 128, :] = xi[:, k * 128 : (k + 1) * 128].T
 
-    def piece_copy(j, src_z, dst_z, kind):
-        if kind < 2:
-            src = ps.at[j, kind, pl.ds(pl.multiple_of(dst_z * MAIN, MAIN), MAIN)]
-        else:
-            src = ps.at[j, dst_z // 2, pl.ds(pl.multiple_of(4 * MAIN + dst_z % 2 * EXTRA, EXTRA), EXTRA)]
-        dst = r1.at[j, src_z, pl.ds(kind * MAIN, MAIN if kind < 2 else EXTRA)]
-        to = device(x, yl, c, yh, dst_z)
-        return remote(src, dst, r1_send.at[j, dst_z, kind], r1_recv.at[j, src_z, kind], to)
+    sides = {(0, 0): 1, (0, -1): 1, (0, 1): -1, (1, 0): -1, (1, -1): 1, (1, 1): -1, (0, 2): 1, (1, 2): -1}
 
     def block_of(i, dr):
         return i * 4 + (x + dr + 4) % 4
 
+    def relay_copy(i, dr):
+        block, side = block_of(i, dr), sides[(i, dr)]
+        src = ps.at[block, (z + 2) % 4]
+        return remote(src, rl.at[block], rl_send.at[block], rl_recv.at[block], zp if side == 1 else zm)
+
+    def piece_copy(i, dr, merged):
+        block, side = block_of(i, dr), sides[(i, dr)]
+        src = mg.at[block] if merged else ps.at[block, (z - side + 4) % 4]
+        to = zp if (side == 1) == merged else zm
+        k = int(merged)
+        return remote(src, r1.at[block, k], r1_send.at[block, k], r1_recv.at[block, k], to)
+
     def gram(i, dr, h):
-        j, block = chip_at(dr, 0), block_of(i, dr)
+        j, block, side = chip_at(dr, 0), block_of(i, dr), sides[(i, dr)]
         part = jnp.dot(xs[j, h * HALF : (h + 1) * HALF, :], xt[i], preferred_element_type=jnp.float32)
-        ps[block, h] = part.astype(jnp.bfloat16)
-        for dz in (2, 1, 3):
-            piece_copy(block, z, (z + dz) % 4, h).start()
-        for piece in (2 * h, 2 * h + 1):
-
-            @pl.when(piece != z)
-            def _(piece=piece):
-                piece_copy(block, z, piece, 2).start()
+        ps[block, 2 * h : 2 * h + 2] = part.astype(jnp.bfloat16).reshape(2, PIECE, CHIP)
+
+        @pl.when((z + 2) % 4 // 2 == h)
+        def _():
+            relay_copy(i, dr).start()
+
+        @pl.when((z - side + 4) % 4 // 2 == h)
+        def _():
+            piece_copy(i, dr, False).start()
+
+    def relay(i, dr):
+        block, side = block_of(i, dr), sides[(i, dr)]
+        relay_copy(i, dr).wait_recv()
+        total = rl[block].astype(jnp.float32) + ps[block, (z + side + 4) % 4].astype(jnp.float32)
+        mg[block] = total.astype(jnp.bfloat16)
+        piece_copy(i, dr, True).start()
 
     def sum_copy(i, xj, slot, to):
         return remote(s_send.at[i, xj], s_recv.at[slot, xj], r2_send.at[i, xj], r2_recv.at[slot, xj], to)
@@ -183,14 +191,10 @@
 
     def reduce(i, dr):
         block = block_of(i, dr)
-        own_rows = [ps[block, h, pl.ds(pl.multiple_of(z * MAIN, MAIN), MAIN)] for h in range(2)]
-        own_rows.append(ps[block, z // 2, pl.ds(pl.multiple_of(4 * MAIN + z % 2 * EXTRA, EXTRA), EXTRA)])
-        total = jnp.concatenate(own_rows, axis=0).astype(jnp.float32)
-        for dz in (1, 3, 2):
-            src_z = (z + dz) % 4
-            for kind in range(3):
-                piece_copy(block, src_z, src_z, kind).wait_recv()
-            total = total + r1[block, src_z].astype(jnp.float32)
+        total = ps[block, z].astype(jnp.float32)
+        for merged in (False, True):
+            piece_copy(i, dr, merged).wait_recv()
+            total = total + r1[block, int(merged)].astype(jnp.float32)
         xj = (x + dr + 4) % 4
         if i == 0:
 
@@ -278,8 +282,7 @@
         gr.arrive(0, 1, k)
 
     def far_of(k):
-        gr.arrive(2, 0, k)
-        for arrive in (arrive_l, gr.arrive):
+        for arrive in (gr.arrive, arrive_l):
             arrive(-1, 1, k)
             arrive(1, 1, k)
         arrive_l(2, 0, k)
@@ -290,12 +293,14 @@
     passed = []
     for h in range(2):
         gx.arrive(-1, 0, h)
-        gx.arrive(1, 0, h)
+        gx.arrive(1, 0, 1 - h)
         gx.arrive(0, 1, h)
         passed.append(pass_pair(h))
         gram(0, -1, h)
-        gram(0, 1, h)
+        gram(0, 1, 1 - h)
         if h == 0:
+            relay(0, 0)
+        else:
             reduce(0, 0)
     for h in range(2):
         gx.spread(h)
@@ -305,32 +310,32 @@
         passed[h][1].wait()
     for k in range(COLS // 128):
         cols = slice(k * 128, (k + 1) * 128)
-        blocks = []
-        for lane in range(2):
-            for piece in range(4):
-                for first in (MAIN * piece, HALF + MAIN * piece):
-                    blocks.append(xq[lane, first : first + MAIN, cols])
-                first = piece // 2 * HALF + 4 * MAIN + piece % 2 * EXTRA
-                blocks.append(xq[lane, first : first + EXTRA, cols])
-        xt[1, cols, :] = jnp.concatenate(blocks, axis=0).T
+        xt[1, cols, :] = xq[:, :, cols].reshape(CHIP, 128).T
+    relay(0, -1)
+    relay(0, 1)
     for dr in (0, -1, 1):
         for h in range(2):
             gram(1, dr, h)
     for h in range(2):
         gx.arrive(2, 0, h)
-        for i in range(2):
+    for i in range(2):
+        for h in range(2):
             gram(i, 2, h)
+    for dr in (0, -1, 1):
+        relay(1, dr)
     reduce(0, -1)
     reduce(0, 1)
     reduce(1, 0)
     finish_sum(0)
+    relay(0, 2)
+    relay(1, 2)
     reduce(1, -1)
     finish_sum(1)
     reduce(1, 1)
     finish_sum(2)
-    near_of(0)
     reduce(0, 2)
     reduce(1, 2)
+    near_of(0)
     finish_sum(3)
     near_of(1)
     far_of(0)
@@ -340,97 +345,106 @@
     far_of(2)
     far_of(3)
     for k in range(4):
+        gr.arrive(2, 0, k)
         gr.arrive(2, 1, k)
     for h in range(2):
         gx.arrive(-1, 1, h)
         gx.arrive(1, 1, h)
 
-    def square(j):
-        left = rt[j].reshape(ROWS, CHIP)
+    def square(j, rows):
+        left = rt[j, rows].reshape(-1, CHIP)
         right = ls[j].reshape(CHIP, CHIP)
         return jnp.dot(left, right, preferred_element_type=jnp.float32)
 
     for dr in (0, -1, 1, 2):
         for k in range(4):
             from_core(dr, 0, k)
-    total = square(yh * 4)
-    for k in range(1, 4):
-        total = total + square(yh * 4 + k)
+    for h in range(2):
+        rows = slice(2 * h, 2 * h + 2)
+        total = square(yh * 4, rows)
+        for k in range(1, 4):
+            total = total + square(yh * 4 + k, rows)
+        sq[rows] = total.reshape(2, PIECE, CHIP)
     for k in range(4):
         arrive_l(2, 1, k)
     for dr in (0, -1, 1, 2):
         for k in range(4):
             from_core(dr, 1, k)
-    for k in range(4):
-        total = total + square((1 - yh) * 4 + k)
-    mixing = (COEF_B * gf[...].reshape(ROWS, CHIP) + COEF_C * total).astype(jnp.bfloat16)
-    mixing = mixing.reshape(4, PIECE, CHIP)
-    for xj in range(4):
-        ms[yh * 4 + xj, z] = mixing[xj]
     def mix_slot(dr, dp, h):
         return ms.at[pl.ds(((yh + dp) % 2) * 4 + h * 2, 2), (z + dr + 4) % 4]
 
     gm = Gather(mix_slot, zp, zm, yq, m_send, m_recv, True)
-    gm.begin(0)
-    gm.begin(1)
-
-    def rows_of(side, at, cols):
-        blocks = []
+    for h in range(2):
+        rows = slice(2 * h, 2 * h + 2)
+        total = sq[rows].reshape(HALF, CHIP)
         for k in range(4):
-            for h in range(2):
-                blocks.append(xs[side + k, pl.ds(pl.multiple_of(h * HALF + at * MAIN, MAIN), MAIN), cols])
-            extra = at // 2 * HALF + 4 * MAIN + at % 2 * EXTRA
-            blocks.append(xs[side + k, pl.ds(pl.multiple_of(extra, EXTRA), EXTRA), cols])
-        return jnp.concatenate(blocks, axis=0)
+            total = total + square((1 - yh) * 4 + k, rows)
+        mixing = COEF_B * gf[rows].reshape(HALF, CHIP) + COEF_C * total
+        ms[pl.ds(yh * 4 + 2 * h, 2), z] = mixing.astype(jnp.bfloat16).reshape(2, PIECE, CHIP)
+        if h == 0:
+            gm.begin(0, ("plus", "pair"))
+        else:
+            gm.begin(1, ("minus", "plus", "pair"))
+            gm.begin(0, ("minus",))
 
     def turn(dr, dp, slot):
         side, at = ((yh + dp) % 2) * 4, (z + dr + 4) % 4
         mt[slot] = ms[pl.ds(side, 4), at].reshape(ROWS, CHIP).T
 
-    def product(dr, dp, slot, rows, first=False):
+    def product(dr, dp, slot, rows, n, first=False):
         side, at = ((yh + dp) % 2) * 4, (z + dr + 4) % 4
-        for n in range(3):
-            cols = pl.ds(n * 384, 384)
-            part = jnp.dot(mt[slot, rows, :], rows_of(side, at, cols), preferred_element_type=jnp.float32)
-            zs[rows, cols] = part if first else zs[rows, cols] + part
+        cols = pl.ds(n * 384, 384)
+        at_rows = pl.ds(pl.multiple_of(at * PIECE, 16), PIECE)
+        right = xs[pl.ds(side, 4), at_rows, cols].reshape(ROWS, 384)
+        part = jnp.dot(mt[slot, rows, :], right, preferred_element_type=jnp.float32)
+        zs[rows, cols] = part if first else zs[rows, cols] + part
 
     every = slice(None)
+    for h in range(2):
+        gm.arrive(-1, 0, h)
+        gm.arrive(1, 0, 1 - h)
+        gm.arrive(0, 1, h)
     for h in range(2):
         gx.arrive(2, 1, h)
     turn(0, 0, 0)
-    product(0, 0, 0, every, True)
-    for h in range(2):
-        gm.arrive(-1, 0, h)
-        gm.arrive(1, 0, h)
-        gm.arrive(0, 1, h)
+    for n in range(3):
+        product(0, 0, 0, every, n, True)
+    for h in range(2):
+        gm.arrive(-1, 1, h)
+        gm.arrive(1, 1, 1 - h)
     for h in range(2):
         gm.arrive(2, 0, h)
     for place in near + ((2, 0),):
         turn(*place, 0)
-        product(*place, 0, every)
+        for n in range(3):
+            product(*place, 0, every, n)
     for k, place in enumerate(far):
-        for h in range(2):
-            gm.arrive(*place, h)
+        if place == (2, 1):
+            for h in range(2):
+                gm.arrive(*place, h)
         turn(*place, k)
-        product(*place, k, theirs)
-    last = remote(zs.at[theirs], zr, z_send, z_recv, core)
-    last.start()
-    for k, place in enumerate(far):
-        product(*place, k, mine)
-    last.wait_recv()
-    total = zs[mine, :] + zr[...]
-    for h in range(2):
-        for first, count, piece, at in spans(h):
-            out_ref[pl.ds(h * HALF + first, count), :] = total[piece * PIECE + at : piece * PIECE + at + count]
-
-    for copy in lanes + [swap, last] + [over for over, _ in passed]:
+    last = []
+    for n in range(3):
+        for k, place in enumerate(far):
+            product(*place, k, theirs, n)
+        zb[n] = zs[theirs, pl.ds(n * 384, 384)].astype(jnp.bfloat16)
+        last.append(remote(zb.at[n], zr.at[n], z_send.at[n], z_recv.at[n], core))
+        last[n].start()
+    for n in range(3):
+        for k, place in enumerate(far):
+            product(*place, k, mine, n)
+        last[n].wait_recv()
+        cols = pl.ds(n * 384, 384)
+        out_ref[:, cols] = zs[mine, cols] + zr[n].astype(jnp.float32)
+
+    for copy in lanes + [swap] + last + [over for over, _ in passed]:
         copy.wait_send()
     for gather in (gx, gr, gl, gm):
         gather.finish()
-    for j in range(8):
-        for dz in (1, 2, 3):
-            for kind in range(3):
-                piece_copy(j, z, (z + dz) % 4, kind).wait_send()
+    for place in sides:
+        relay_copy(*place).wait_send()
+        piece_copy(*place, False).wait_send()
+        piece_copy(*place, True).wait_send()
     for xj in range(4):
         sum_copy(1, xj, 0, yp).wait_send()
 
@@ -454,23 +468,27 @@
             pltpu.VMEM((CHIP, COLS), half),
             pltpu.VMEM((2, ROWS, COLS), half),
             pltpu.VMEM((2, COLS, CHIP), half),
-            pltpu.VMEM((8, 2, HALF, CHIP), half),
             pltpu.VMEM((8, 4, PIECE, CHIP), half),
+            pltpu.VMEM((8, PIECE, CHIP), half),
+            pltpu.VMEM((8, PIECE, CHIP), half),
+            pltpu.VMEM((8, 2, PIECE, CHIP), half),
             pltpu.VMEM((4, PIECE, CHIP), full),
             pltpu.VMEM((2, 4, PIECE, CHIP), half),
             pltpu.VMEM((2, 4, PIECE, CHIP), half),
+            pltpu.VMEM((4, PIECE, CHIP), full),
             pltpu.VMEM((4, PIECE, CHIP), full),
             pltpu.VMEM((8, 4, PIECE, CHIP), half),
             pltpu.VMEM((8, 2, 4, PIECE, CHIP), half),
             pltpu.VMEM((8, 4, PIECE, CHIP), half),
             pltpu.VMEM((3, CHIP, ROWS), half),
             pltpu.VMEM((CHIP, COLS), full),
-            pltpu.VMEM((ROWS, COLS), full),
+            pltpu.VMEM((3, ROWS, 384), half),
+            pltpu.VMEM((3, ROWS, 384), half),
             dma((4,)), dma((14,)), dma((16,)), dma(()), dma(()), dma((2,)), dma((2,)), dma((2,)),
-            dma((8, 4, 3)), dma((8, 4, 3)), dma((2, 4)), dma((2, 4)),
+            dma((8,)), dma((8,)), dma((8, 2)), dma((8, 2)), dma((2, 4)), dma((2, 4)),
             dma((28,)), dma((32,)), dma((28,)), dma((32,)),
             dma((32,)), dma((32,)), dma((14,)), dma((16,)),
-            dma(()), dma(()),
+            dma((3,)), dma((3,)),
         ],
         name="muon",
         compiler_params=pltpu.CompilerParams(

time: 127 us -> 133 us (1.047)
  Pallas kernels: 123 us -> 129 us
    pallas_call x1, Pallas kernels: 123 us -> 129 us  [local(): pl.pallas_call(kernel, out_shape=jax.ShapeDtypeStruct((ROWS, COLS), full)...]
where the time goes in v5:
time: 133 us
  Pallas kernels  129 us (97%)
  other arithmetic  3.35 us (3%)
    pallas_call x1, Pallas kernels, local(): pl.pallas_call(kernel, out_shape=jax.ShapeDtypeStruct((ROWS, COLS), full)...  129 us
    mul x1, other arithmetic, local(): return (new_momentum, SCALE * (COEF_A * nesterov + product))  3.35 us

profile of v5, /device:TPU:1, one launch (start us, length us, event | category | flops | bytes accessed | tf_op | source)
XLA Modules:
  0.0 132.9 jit_solution(8284725782073449646)
XLA Ops:
  0.6 0.0 copy-start.1
  0.6 0.0 copy-start
  0.6 128.9 %muon.1 = f32[320,1152]{1,0:T(8,128)} custom-call(f32[320,1152]{1,0:T(8,128)} %g_hbm.1, f32[320,1152]{1,0:T(8,128)} %m_hbm.1), custom_call_target="tpu_custom_call" | custom-call | tf_op jit(solution)/shard_map/muon/pallas_call | solution.py:459
  129.5 0.0 copy-done.1
  129.5 0.0 copy-done
  129.6 3.3 %add_multiply_fusion = (f32[320,1152]{1,0:T(8,128)}, f32[320,1152]{1,0:T(8,128)}) fusion(f32[320,1152]{1,0:T(8,128)} %muon.1, f32[320,1152]{1,0:T(8,128)S(1)} %copy-done, f32[320,1152]{1,0:T(8,128)S(1)} %copy-done.1), kind=kLoop, calls=%fused_computation | loop fusion | flops 2580480 | bytes 7372800 | tf_op jit(solution)/shard_map/mul | solution.py:500
Async XLA Ops:
  0.6 128.9 %copy-start.1 = (f32[320,1152]{1,0:T(8,128)S(1)}, f32[320,1152]{1,0:T(8,128)}, u32[]{:S(2)}) copy-start(f32[320,1152]{1,0:T(8,128)} %m_hbm.1) | copy-start | bytes 4423684
  0.6 128.9 %copy-start = (f32[320,1152]{1,0:T(8,128)S(1)}, f32[320,1152]{1,0:T(8,128)}, u32[]{:S(2)}) copy-start(f32[320,1152]{1,0:T(8,128)} %g_hbm.1) | copy-start | bytes 4423684

commit v6 on v5

v6 whole, which is shorter than its diff:
```python
import math

import jax
import jax.numpy as jnp
from jax import lax
from jax.experimental import pallas as pl
from jax.experimental.pallas import tpu as pltpu
from jax.sharding import PartitionSpec as P

HIDDEN_SIZE = 9216
MOMENTUM_RATE = 0.95
COEF_A = 3.4445
COEF_B = -4.775
COEF_C = 2.0315
SCALE = math.sqrt(HIDDEN_SIZE)

MESH = pl.DeviceIdType.MESH
ROWS = 320
COLS = 1152
HALF = ROWS // 2
CHIP = 2 * ROWS
PIECE = ROWS // 4
ORDER = (0, -1, 1, 2)
PLACES = {(0, 0): 0, (-1, 0): 1, (1, 0): 2, (2, 0): 3, (0, 1): 4, (-1, 1): 5, (1, 1): 6, (2, 1): 7}


class Gather:
    def __init__(self, slot, plus, minus, pair, send, recv, mode, parts=2, hold=False):
        self.slot, self.plus, self.minus, self.pair = slot, plus, minus, pair
        self.send, self.recv, self.mode = send, recv, mode
        self.parts, self.hold, self.started = parts, hold, []

    def _copy(self, dr, dp, h, to):
        device, ring, other = {"plus": (self.plus, -1, 0), "minus": (self.minus, 1, 0), "pair": (self.pair, 0, 1)}[to]
        there = dr + ring
        there = 2 if there == -2 else there
        place = PLACES[(there, (dp + other) % 2)] * self.parts + h
        ref = self.slot(dr, dp, h)
        copy = pltpu.make_async_remote_copy(
            src_ref=ref,
            dst_ref=ref,
            send_sem=self.send.at[len(self.started)],
            recv_sem=self.recv.at[place],
            device_id=device,
            device_id_type=MESH,
        )
        copy.start()
        self.started.append(copy)

    def begin(self, h, links=("plus", "minus", "pair")):
        for to in links:
            self._copy(0, 0, h, to)

    def spread(self, h):
        if self.mode != "cross" or h % 2 == 1:
            self._copy(0, 1, h, "plus")
        if self.mode != "cross" or h % 2 == 0:
            self._copy(0, 1, h, "minus")

    def arrive(self, dr, dp, h):
        ref = self.slot(dr, dp, h)
        place = PLACES[(dr, dp)] * self.parts + h
        pltpu.make_async_remote_copy(
            src_ref=ref,
            dst_ref=ref,
            send_sem=self.send.at[0],
            recv_sem=self.recv.at[place],
            device_id=self.pair,
            device_id_type=MESH,
        ).wait_recv()
        if (dr, dp) == (0, 1):
            if not self.hold:
                self.spread(h)
        elif (dr, h % 2) in ((-1, 0), (1, 1)) and (dp == 0 or self.mode != "late"):
            self._copy(dr, dp, h, "plus" if dr == -1 else "minus")
            if self.mode == "cross" and dp == 0:
                self._copy(dr, dp, h, "pair")
        elif (dr, dp) == (2, 0) and self.mode == "late":
            self._copy(dr, dp, h, "pair")

    def finish(self):
        for copy in self.started:
            copy.wait_send()


def kernel(
    g_hbm, m_hbm, out_ref,
    g_ref, m_ref, xs, xi, xq, xt, ps, r1, keep, s_send, s_recv, gf, sq, rt, ls, ms, mt, zs, zb, zr,
    in_sem, x_send, x_recv, xc_send, xc_recv, xq_send, xq_recv, xq_sem, r1_send, r1_recv, r2_send, r2_recv,
    rt_send, rt_recv, l_send, l_recv, lc_send, lc_recv, m_send, m_recv, z_send, z_recv,
):
    row, col = lax.axis_index("row"), lax.axis_index("col")
    c, x, yl = row % 2, (row // 2) % 4, row // 8
    z, yh = col % 4, col // 4

    def device(x_, yl_, c_, yh_, z_):
        return ((yl_ * 4 + x_) * 2 + c_, yh_ * 4 + z_)

    core = device(x, yl, 1 - c, yh, z)
    xp, xm = device((x + 1) % 4, yl, c, yh, z), device((x + 3) % 4, yl, c, yh, z)
    zp, zm = device(x, yl, c, yh, (z + 1) % 4), device(x, yl, c, yh, (z + 3) % 4)
    z2 = device(x, yl, c, yh, (z + 2) % 4)
    yp, yq = device(x, 1 - yl, c, yh, z), device(x, yl, c, 1 - yh, z)
    yd = device(x, 1 - yl, c, 1 - yh, z)
    barrier = pltpu.get_barrier_semaphore()
    partners = (core, xp, xm, zp, zm, z2, yp, yq, yd)
    for partner in partners:
        pl.semaphore_signal(barrier, inc=1, device_id=partner, device_id_type=MESH)
    loads = []
    for h in range(2):
        rows = pl.ds(h * HALF, HALF)
        for k, (hbm, ref) in enumerate(((g_hbm, g_ref), (m_hbm, m_ref))):
            load = pltpu.make_async_copy(hbm.at[rows], ref.at[rows], in_sem.at[2 * h + k])
            load.start()
            loads.append(load)

    def remote(src, dst, send, recv, to):
        return pltpu.make_async_remote_copy(
            src_ref=src, dst_ref=dst, send_sem=send, recv_sem=recv, device_id=to, device_id_type=MESH
        )

    def chip_at(dr, dp):
        return ((yl + dp) % 2) * 4 + (x + dr + 4) % 4

    own = chip_at(0, 0)

    gx = Gather(lambda dr, dp, h: xs.at[chip_at(dr, dp), pl.ds(h * HALF, HALF)], xp, xm, yp, x_send, x_recv, "ring", hold=True)
    mine = pl.ds(pl.multiple_of(c * ROWS, 32), ROWS)
    theirs = pl.ds(pl.multiple_of((1 - c) * ROWS, 32), ROWS)
    for h in range(2):
        rows = pl.ds(h * HALF, HALF)
        loads[2 * h].wait()
        loads[2 * h + 1].wait()
        new = MOMENTUM_RATE * m_ref[rows, :] + g_ref[rows, :]
        low = (g_ref[rows, :] + MOMENTUM_RATE * new).astype(jnp.bfloat16)
        xs[own, rows, :] = low
        if h == 0:
            pl.semaphore_wait(barrier, len(partners))
            gx.begin(0, ("plus", "pair"))
        else:
            gx.begin(1, ("minus", "plus", "pair"))
            gx.begin(0, ("minus",))
        xi[pl.ds(pl.multiple_of(c * ROWS + h * HALF, 32), HALF), :] = low
    swap = remote(xi.at[mine], xi.at[mine], xc_send, xc_recv, core)
    swap.start()
    remote(xi.at[theirs], xi.at[theirs], xc_send, xc_recv, core).wait_recv()
    for k in range(COLS // 128):
        xt[0, k * 128 : (k + 1) * 128, :] = xi[:, k * 128 : (k + 1) * 128].T

    def block_of(i, dr):
        return i * 4 + (x + dr + 4) % 4

    def piece_copy(block, dz):
        src = ps.at[block, (z + dz) % 4]
        k = dz - 1
        return remote(src, r1.at[block, k], r1_send.at[block, k], r1_recv.at[block, k], (zp, z2, zm)[k])

    def gram(i, dr, h):
        j, block = chip_at(dr, 0), block_of(i, dr)
        part = jnp.dot(xs[j, h * HALF : (h + 1) * HALF, :], xt[i], preferred_element_type=jnp.float32)
        ps[block, 2 * h : 2 * h + 2] = part.astype(jnp.bfloat16).reshape(2, PIECE, CHIP)
        for dz in (2, 1, 3):

            @pl.when((z + dz) % 4 // 2 == h)
            def _(dz=dz):
                piece_copy(block, dz).start()

    def sum_copy(i, xj, slot):
        to = (yq, yp, yd)[slot]
        return remote(s_send.at[i, xj], s_recv.at[slot, xj], r2_send.at[slot, xj], r2_recv.at[slot, xj], to)

    def reduce(i, dr):
        block = block_of(i, dr)
        total = ps[block, z].astype(jnp.float32)
        for dz in (1, 3, 2):
            piece_copy(block, dz).wait_recv()
            total = total + r1[block, dz - 1].astype(jnp.float32)
        xj = (x + dr + 4) % 4
        s_send[i, xj] = total.astype(jnp.bfloat16)
        if i == 0:
            keep[xj] = total
            sum_copy(0, xj, 0).start()
        else:
            sum_copy(1, xj, 1).start()
            sum_copy(1, xj, 2).start()

    def pass_pair(h):
        rows = pl.ds(h * HALF, HALF)
        src = xs.at[chip_at(0, 1), rows]
        over = remote(src, xq.at[c, rows], xq_send.at[h], xq_recv.at[h], core)
        over.start()
        here = pltpu.make_async_copy(src, xq.at[c, rows], xq_sem.at[h])
        here.start()
        return over, here

    def row_block(dr, dp, k):
        at, side = (x + dr + 4) % 4, (yl + dp + k // 2) % 2
        return side, (at + 2 * (k % 2) + 3 * ((at + yh) % 2)) % 4

    def row_slot(dr, dp, k):
        side, xj = row_block(dr, dp, k)
        return rt.at[chip_at(dr, dp), side * 2 + xj // 2]

    gr = Gather(row_slot, xp, xm, yp, rt_send, rt_recv, "cross", 4)
    parts = ((0, 0), (0, -1), (0, 1), (1, 0), (1, -1), (0, 2), (1, 1), (1, 2))
    lanes, l_sent = [], []

    def l_slot(n, dz, lane):
        i, dr = parts[n]
        return ls.at[chip_at(dr, i), lane, (z + dz + 4) % 4]

    def l_copy(n, dz, side):
        there = {(0, 1): -1, (0, -1): 1, (-1, 1): 2, (1, -1): 2}[(dz, side)]
        ref = l_slot(n, dz, c)
        to = zp if side == 1 else zm
        copy = remote(ref, ref, l_send.at[len(l_sent)], l_recv.at[(there % 4) * 8 + n], to)
        copy.start()
        l_sent.append(copy)

    def to_core(n, dz):
        place = (dz % 4) * 8 + n
        copy = remote(l_slot(n, dz, c), l_slot(n, dz, c), lc_send.at[place], lc_recv.at[place], core)
        copy.start()
        lanes.append(copy)

    def from_core(n, dz):
        place = (dz % 4) * 8 + n
        ref = l_slot(n, dz, 1 - c)
        remote(ref, ref, lc_send.at[place], lc_recv.at[place], core).wait_recv()

    def l_arrive(n, dz):
        ref = l_slot(n, dz, c)
        remote(ref, ref, l_send.at[0], l_recv.at[(dz % 4) * 8 + n], zp).wait_recv()
        if dz == -1 and n % 2 == 0:
            l_copy(n, -1, 1)
        if dz == 1 and n % 2 == 1:
            l_copy(n, 1, -1)
        to_core(n, dz)

    def l_near(n):
        l_arrive(n, -1)
        l_arrive(n, 1)

    def finish_sum(n):
        i, dr = parts[n]
        xj, j = (x + dr + 4) % 4, chip_at(dr, i)
        for slot in (1, 2) if i else (0,):
            ref = s_recv.at[slot, xj]
            remote(ref, ref, r2_send.at[slot, xj], r2_recv.at[slot, xj], yp).wait_recv()
        if i:
            total = s_recv[1, xj].astype(jnp.float32) + s_recv[2, xj].astype(jnp.float32)
        else:
            total = keep[xj] + s_recv[0, xj].astype(jnp.float32)
        gf[j] = total
        ls[j, c, z] = total.astype(jnp.bfloat16)
        l_copy(n, 0, 1)
        l_copy(n, 0, -1)
        to_core(n, 0)

    def r_begin(k):
        side, xj = row_block(0, 0, k)
        rt[own, side * 2 + xj // 2] = ls[side * 4 + xj, c, z]
        gr.begin(k)

    def r_near(k):
        gr.arrive(-1, 0, k)
        gr.arrive(1, 0, k)
        gr.arrive(0, 1, k)

    def r_far(k):
        gr.arrive(-1, 1, k)
        gr.arrive(1, 1, k)

    near, far = ((-1, 0), (1, 0), (0, 1)), ((-1, 1), (1, 1), (2, 1))
    gram(0, 0, 0)
    gram(0, 0, 1)
    passed = []
    for h in range(2):
        gx.arrive(-1, 0, h)
        gx.arrive(1, 0, 1 - h)
        gx.arrive(0, 1, h)
        passed.append(pass_pair(h))
        gram(0, -1, h)
        gram(0, 1, 1 - h)
        if h == 0:
            reduce(0, 0)
    for h in range(2):
        gx.spread(h)
    finish_sum(0)
    for h in range(2):
        ref = xq.at[1 - c, pl.ds(h * HALF, HALF)]
        remote(ref, ref, xq_send.at[h], xq_recv.at[h], core).wait_recv()
        passed[h][1].wait()
    for k in range(COLS // 128):
        cols = slice(k * 128, (k + 1) * 128)
        xt[1, cols, :] = xq[:, :, cols].reshape(CHIP, 128).T
    for dr in (0, -1, 1):
        for h in range(2):
            gram(1, dr, h)
    for h in range(2):
        gx.arrive(2, 0, h)
    for i in range(2):
        for h in range(2):
            gram(i, 2, h)
    reduce(0, -1)
    reduce(0, 1)
    reduce(1, 0)
    reduce(1, -1)
    reduce(1, 1)
    l_near(0)
    finish_sum(1)
    finish_sum(2)
    r_begin(0)
    reduce(0, 2)
    reduce(1, 2)
    finish_sum(3)
    finish_sum(4)
    r_begin(2)
    l_near(1)
    l_near(2)
    finish_sum(5)
    r_begin(1)
    finish_sum(6)
    finish_sum(7)
    r_begin(3)
    l_near(3)
    l_near(4)
    r_near(0)
    l_near(5)
    r_near(2)
    l_near(6)
    r_near(1)
    r_far(0)
    r_far(2)
    l_near(7)
    r_near(3)
    r_far(1)
    r_far(3)
    for n in range(8):
        l_arrive(n, 2)
    for k in range(4):
        gr.arrive(2, 0, k)
        gr.arrive(2, 1, k)
    for h in range(2):
        gx.arrive(-1, 1, h)
        gx.arrive(1, 1, h)

    def square(j, rows):
        left = rt[j, rows].reshape(-1, CHIP)
        right = ls[j].reshape(CHIP, CHIP)
        return jnp.dot(left, right, preferred_element_type=jnp.float32)

    for n in range(8):
        for dz in (0, -1, 1, 2):
            if parts[n][0] == 0:
                from_core(n, dz)
    for h in range(2):
        rows = slice(2 * h, 2 * h + 2)
        total = square(yl * 4, rows)
        for k in range(1, 4):
            total = total + square(yl * 4 + k, rows)
        sq[rows] = total.reshape(2, PIECE, CHIP)
    for n in range(8):
        for dz in (0, -1, 1, 2):
            if parts[n][0] == 1:
                from_core(n, dz)

    def mix_slot(dr, dp, h):
        return ms.at[h, :, (yh + dp) % 2, (z + dr + 4) % 4]

    gm = Gather(mix_slot, zp, zm, yq, m_send, m_recv, "cross")
    for h in range(2):
        rows = slice(2 * h, 2 * h + 2)
        total = sq[rows].reshape(HALF, CHIP)
        for k in range(4):
            total = total + square((1 - yl) * 4 + k, rows)
        gram_rows = jnp.concatenate([gf[h * 4 + yh], gf[h * 4 + 2 + yh]], axis=0)
        mixing = (COEF_B * gram_rows + COEF_C * total).astype(jnp.bfloat16)
        ms[h, 0, yh, z] = mixing[:PIECE]
        ms[h, 1, yh, z] = mixing[PIECE:]
        if h == 0:
            gm.begin(0, ("plus", "pair"))
        else:
            gm.begin(1, ("minus", "plus", "pair"))
            gm.begin(0, ("minus",))

    def turn(dr, dp, slot):
        mt[slot] = ms[:, :, (yh + dp) % 2, (z + dr + 4) % 4].reshape(ROWS, CHIP).T

    def product(dr, dp, slot, rows, n, first=False):
        side, at = (yh + dp) % 2, (z + dr + 4) % 4
        cols = pl.ds(n * 384, 384)
        at_rows = pl.ds(pl.multiple_of(at * PIECE, 16), PIECE)
        right = jnp.concatenate([xs[2 * k + side, at_rows, cols] for k in range(4)], axis=0)
        part = jnp.dot(mt[slot, rows, :], right, preferred_element_type=jnp.float32)
        zs[rows, cols] = part if first else zs[rows, cols] + part

    every = slice(None)
    for h in range(2):
        gm.arrive(-1, 0, h)
        gm.arrive(1, 0, 1 - h)
        gm.arrive(0, 1, h)
    for h in range(2):
        gx.arrive(2, 1, h)
    turn(0, 0, 0)
    for n in range(3):
        product(0, 0, 0, every, n, True)
    for h in range(2):
        gm.arrive(-1, 1, h)
        gm.arrive(1, 1, 1 - h)
    for h in range(2):
        gm.arrive(2, 0, h)
    for place in near + ((2, 0),):
        turn(*place, 0)
        for n in range(3):
            product(*place, 0, every, n)
    for k, place in enumerate(far):
        if place == (2, 1):
            for h in range(2):
                gm.arrive(*place, h)
        turn(*place, k)
    last = []
    for n in range(3):
        for k, place in enumerate(far):
            product(*place, k, theirs, n)
        zb[n] = zs[theirs, pl.ds(n * 384, 384)].astype(jnp.bfloat16)
        last.append(remote(zb.at[n], zr.at[n], z_send.at[n], z_recv.at[n], core))
        last[n].start()
    for n in range(3):
        for k, place in enumerate(far):
            product(*place, k, mine, n)
        last[n].wait_recv()
        cols = pl.ds(n * 384, 384)
        out_ref[:, cols] = zs[mine, cols] + zr[n].astype(jnp.float32)

    for copy in lanes + l_sent + [swap] + last + [over for over, _ in passed]:
        copy.wait_send()
    for gather in (gx, gr, gm):
        gather.finish()
    for block in range(8):
        for dz in (1, 2, 3):
            piece_copy(block, dz).wait_send()
    for xj in range(4):
        for slot in range(3):
            sum_copy(min(slot, 1), xj, slot).wait_send()


def local(gradient, momentum):
    half, full = jnp.bfloat16, jnp.float32
    dma = pltpu.SemaphoreType.DMA
    product = pl.pallas_call(
        kernel,
        out_shape=jax.ShapeDtypeStruct((ROWS, COLS), full),
        in_specs=[pl.BlockSpec(memory_space=pl.ANY)] * 2,
        out_specs=pl.BlockSpec(memory_space=pltpu.VMEM),
        scratch_shapes=[
            pltpu.VMEM((ROWS, COLS), full),
            pltpu.VMEM((ROWS, COLS), full),
            pltpu.VMEM((8, ROWS, COLS), half),
            pltpu.VMEM((CHIP, COLS), half),
            pltpu.VMEM((2, ROWS, COLS), half),
            pltpu.VMEM((2, COLS, CHIP), half),
            pltpu.VMEM((8, 4, PIECE, CHIP), half),
            pltpu.VMEM((8, 3, PIECE, CHIP), half),
            pltpu.VMEM((4, PIECE, CHIP), full),
            pltpu.VMEM((2, 4, PIECE, CHIP), half),
            pltpu.VMEM((3, 4, PIECE, CHIP), half),
            pltpu.VMEM((8, PIECE, CHIP), full),
            pltpu.VMEM((4, PIECE, CHIP), full),
            pltpu.VMEM((8, 4, PIECE, CHIP), half),
            pltpu.VMEM((8, 2, 4, PIECE, CHIP), half),
            pltpu.VMEM((2, 2, 2, 4, PIECE, CHIP), half),
            pltpu.VMEM((3, CHIP, ROWS), half),
            pltpu.VMEM((CHIP, COLS), full),
            pltpu.VMEM((3, ROWS, 384), half),
            pltpu.VMEM((3, ROWS, 384), half),
            dma((4,)), dma((14,)), dma((16,)), dma(()), dma(()), dma((2,)), dma((2,)), dma((2,)),
            dma((8, 3)), dma((8, 3)), dma((3, 4)), dma((3, 4)),
            dma((28,)), dma((32,)), dma((28,)), dma((32,)),
            dma((32,)), dma((32,)), dma((14,)), dma((16,)),
            dma((3,)), dma((3,)),
        ],
        name="muon",
        compiler_params=pltpu.CompilerParams(
            collective_id=0, has_side_effects=True, vmem_limit_bytes=60 * 2**20
        ),
    )(gradient, momentum)
    new_momentum = MOMENTUM_RATE * momentum + gradient
    nesterov = gradient + MOMENTUM_RATE * new_momentum
    return new_momentum, SCALE * (COEF_A * nesterov + product)


def solution(mesh):
    specs = (P("row", "col"), P("row", "col"))
    return jax.shard_map(local, mesh=mesh, in_specs=specs, out_specs=specs, check_vma=False)
```

time: 133 us -> 127 us (0.955)
  Pallas kernels: 129 us -> 123 us
    pallas_call x1, Pallas kernels: 129 us -> 123 us  [local(): pl.pallas_call(kernel, out_shape=jax.ShapeDtypeStruct((ROWS, COLS), full)...]
where the time goes in v6:
time: 127 us
  Pallas kernels  123 us (97%)
  other arithmetic  3.35 us (3%)
    pallas_call x1, Pallas kernels, local(): pl.pallas_call(kernel, out_shape=jax.ShapeDtypeStruct((ROWS, COLS), full)...  123 us
    mul x1, other arithmetic, local(): return (new_momentum, SCALE * (COEF_A * nesterov + product))  3.35 us

profile of v6, /device:TPU:1, one launch (start us, length us, event | category | flops | bytes accessed | tf_op | source)
XLA Modules:
  0.0 126.7 jit_solution(221800026929644089)
XLA Ops:
  0.6 0.0 copy-start.1
  0.6 0.0 copy-start
  0.6 122.7 %muon.1 = f32[320,1152]{1,0:T(8,128)} custom-call(f32[320,1152]{1,0:T(8,128)} %g_hbm.1, f32[320,1152]{1,0:T(8,128)} %m_hbm.1), custom_call_target="tpu_custom_call" | custom-call | tf_op jit(solution)/shard_map/muon/pallas_call | solution.py:451
  123.3 0.0 copy-done.1
  123.3 0.0 copy-done
  123.4 3.3 %add_multiply_fusion = (f32[320,1152]{1,0:T(8,128)}, f32[320,1152]{1,0:T(8,128)}) fusion(f32[320,1152]{1,0:T(8,128)} %muon.1, f32[320,1152]{1,0:T(8,128)S(1)} %copy-done, f32[320,1152]{1,0:T(8,128)S(1)} %copy-done.1), kind=kLoop, calls=%fused_computation | loop fusion | flops 2580480 | bytes 7372800 | tf_op jit(solution)/shard_map/mul | solution.py:490
Async XLA Ops:
  0.6 122.7 %copy-start.1 = (f32[320,1152]{1,0:T(8,128)S(1)}, f32[320,1152]{1,0:T(8,128)}, u32[]{:S(2)}) copy-start(f32[320,1152]{1,0:T(8,128)} %m_hbm.1) | copy-start | bytes 4423684
  0.6 122.7 %copy-start = (f32[320,1152]{1,0:T(8,128)S(1)}, f32[320,1152]{1,0:T(8,128)}, u32[]{:S(2)}) copy-start(f32[320,1152]{1,0:T(8,128)} %g_hbm.1) | copy-start | bytes 4423684

commit v7 on v6

--- a/solution.py
+++ b/solution.py
@@ -20,7 +20,7 @@
 HALF = ROWS // 2
 CHIP = 2 * ROWS
 PIECE = ROWS // 4
-ORDER = (0, -1, 1, 2)
+RELAY = {(0, 1): 1, (1, -1): 1, (1, 1): -1, (0, 2): 1, (1, 2): -1}
 PLACES = {(0, 0): 0, (-1, 0): 1, (1, 0): 2, (2, 0): 3, (0, 1): 4, (-1, 1): 5, (1, 1): 6, (2, 1): 7}
 
 
@@ -85,8 +85,8 @@
 
 def kernel(
     g_hbm, m_hbm, out_ref,
-    g_ref, m_ref, xs, xi, xq, xt, ps, r1, keep, s_send, s_recv, gf, sq, rt, ls, ms, mt, zs, zb, zr,
-    in_sem, x_send, x_recv, xc_send, xc_recv, xq_send, xq_recv, xq_sem, r1_send, r1_recv, r2_send, r2_recv,
+    g_ref, m_ref, xs, xi, xq, xt, ps, rl, mg, r1, keep, s_send, s_recv, gf, sq, rt, ls, ms, mt, zs, zb, zr,
+    in_sem, x_send, x_recv, xc_send, xc_recv, xq_send, xq_recv, xq_sem, rl_send, rl_recv, r1_send, r1_recv, r2_send, r2_recv,
     rt_send, rt_recv, l_send, l_recv, lc_send, lc_recv, m_send, m_recv, z_send, z_recv,
 ):
     row, col = lax.axis_index("row"), lax.axis_index("col")
@@ -150,20 +150,43 @@
     def block_of(i, dr):
         return i * 4 + (x + dr + 4) % 4
 
-    def piece_copy(block, dz):
-        src = ps.at[block, (z + dz) % 4]
+    def piece_copy(block, dz, src=None):
+        src = ps.at[block, (z + dz) % 4] if src is None else src
         k = dz - 1
         return remote(src, r1.at[block, k], r1_send.at[block, k], r1_recv.at[block, k], (zp, z2, zm)[k])
+
+    def relay_copy(i, dr):
+        block = block_of(i, dr)
+        to = zp if RELAY[(i, dr)] == 1 else zm
+        return remote(ps.at[block, (z + 2) % 4], rl.at[block], rl_send.at[block], rl_recv.at[block], to)
+
+    def pieces_of(i, dr):
+        block = block_of(i, dr)
+        if (i, dr) not in RELAY:
+            return [(dz, piece_copy(block, dz)) for dz in (2, 1, 3)]
+        back = 4 - RELAY[(i, dr)] if RELAY[(i, dr)] == 1 else 1
+        return [(2, relay_copy(i, dr)), (back, piece_copy(block, back))]
 
     def gram(i, dr, h):
         j, block = chip_at(dr, 0), block_of(i, dr)
         part = jnp.dot(xs[j, h * HALF : (h + 1) * HALF, :], xt[i], preferred_element_type=jnp.float32)
         ps[block, 2 * h : 2 * h + 2] = part.astype(jnp.bfloat16).reshape(2, PIECE, CHIP)
-        for dz in (2, 1, 3):
+        for dz, copy in pieces_of(i, dr):
 
             @pl.when((z + dz) % 4 // 2 == h)
-            def _(dz=dz):
-                piece_copy(block, dz).start()
+            def _(copy=copy):
+                copy.start()
+
+    def onward(i, dr):
+        block, dz = block_of(i, dr), RELAY[(i, dr)] % 4
+        return piece_copy(block, dz, mg.at[block])
+
+    def relay(i, dr):
+        block = block_of(i, dr)
+        relay_copy(i, dr).wait_recv()
+        total = rl[block].astype(jnp.float32) + ps[block, (z + RELAY[(i, dr)] + 4) % 4].astype(jnp.float32)
+        mg[block] = total.astype(jnp.bfloat16)
+        onward(i, dr).start()
 
     def sum_copy(i, xj, slot):
         to = (yq, yp, yd)[slot]
@@ -172,7 +195,7 @@
     def reduce(i, dr):
         block = block_of(i, dr)
         total = ps[block, z].astype(jnp.float32)
-        for dz in (1, 3, 2):
+        for dz in (1, 3) if (i, dr) in RELAY else (1, 3, 2):
             piece_copy(block, dz).wait_recv()
             total = total + r1[block, dz - 1].astype(jnp.float32)
         xj = (x + dr + 4) % 4
@@ -236,10 +259,6 @@
         if dz == 1 and n % 2 == 1:
             l_copy(n, 1, -1)
         to_core(n, dz)
-
-    def l_near(n):
-        l_arrive(n, -1)
-        l_arrive(n, 1)
 
     def finish_sum(n):
         i, dr = parts[n]
@@ -262,108 +281,145 @@
         rt[own, side * 2 + xj // 2] = ls[side * 4 + xj, c, z]
         gr.begin(k)
 
-    def r_near(k):
-        gr.arrive(-1, 0, k)
-        gr.arrive(1, 0, k)
-        gr.arrive(0, 1, k)
-
-    def r_far(k):
-        gr.arrive(-1, 1, k)
-        gr.arrive(1, 1, k)
-
-    near, far = ((-1, 0), (1, 0), (0, 1)), ((-1, 1), (1, 1), (2, 1))
+    def load_pair():
+        for h in range(2):
+            ref = xq.at[1 - c, pl.ds(h * HALF, HALF)]
+            remote(ref, ref, xq_send.at[h], xq_recv.at[h], core).wait_recv()
+            passed[h][1].wait()
+        for k in range(COLS // 128):
+            cols = slice(k * 128, (k + 1) * 128)
+            xt[1, cols, :] = xq[:, :, cols].reshape(CHIP, 128).T
+
+    passed = []
+    gram(0, 0, 1)
+    gx.arrive(-1, 0, 0)
+    gram(0, -1, 0)
+    gx.arrive(1, 0, 1)
     gram(0, 0, 0)
-    gram(0, 0, 1)
-    passed = []
-    for h in range(2):
-        gx.arrive(-1, 0, h)
-        gx.arrive(1, 0, 1 - h)
-        gx.arrive(0, 1, h)
-        passed.append(pass_pair(h))
-        gram(0, -1, h)
-        gram(0, 1, 1 - h)
-        if h == 0:
-            reduce(0, 0)
-    for h in range(2):
-        gx.spread(h)
+    gram(0, 1, 1)
+    gx.arrive(0, 1, 0)
+    passed.append(pass_pair(0))
+    gx.arrive(-1, 0, 1)
+    gram(0, -1, 1)
+    gx.arrive(1, 0, 0)
+    gx.arrive(0, 1, 1)
+    passed.append(pass_pair(1))
+    gram(0, 1, 0)
+    load_pair()
+    gram(1, 0, 0)
+    gx.spread(1)
+    gram(1, 1, 1)
+    gram(1, -1, 1)
+    gram(1, 0, 1)
+    reduce(0, 0)
+    gx.arrive(2, 0, 0)
+    gram(1, -1, 0)
+    gx.arrive(2, 0, 1)
+    gx.spread(0)
+    relay(0, 1)
+    gram(0, 2, 0)
+    gram(0, 2, 1)
+    gram(1, 2, 1)
+    reduce(0, -1)
+    gram(1, 1, 0)
+    relay(1, -1)
+    gram(1, 2, 0)
+    reduce(1, 0)
+    reduce(0, 1)
     finish_sum(0)
-    for h in range(2):
-        ref = xq.at[1 - c, pl.ds(h * HALF, HALF)]
-        remote(ref, ref, xq_send.at[h], xq_recv.at[h], core).wait_recv()
-        passed[h][1].wait()
-    for k in range(COLS // 128):
-        cols = slice(k * 128, (k + 1) * 128)
-        xt[1, cols, :] = xq[:, :, cols].reshape(CHIP, 128).T
-    for dr in (0, -1, 1):
-        for h in range(2):
-            gram(1, dr, h)
-    for h in range(2):
-        gx.arrive(2, 0, h)
-    for i in range(2):
-        for h in range(2):
-            gram(i, 2, h)
-    reduce(0, -1)
-    reduce(0, 1)
-    reduce(1, 0)
+    relay(1, 2)
+    relay(1, 1)
+    gx.arrive(1, 1, 1)
+    relay(0, 2)
+    finish_sum(1)
+    r_begin(0)
+    gx.arrive(-1, 1, 0)
     reduce(1, -1)
+    finish_sum(2)
+    finish_sum(3)
+    reduce(1, 2)
     reduce(1, 1)
-    l_near(0)
-    finish_sum(1)
-    finish_sum(2)
-    r_begin(0)
-    reduce(0, 2)
-    reduce(1, 2)
-    finish_sum(3)
     finish_sum(4)
     r_begin(2)
-    l_near(1)
-    l_near(2)
+    reduce(0, 2)
+    finish_sum(6)
+    finish_sum(7)
+    l_arrive(0, -1)
+    r_begin(3)
+    l_arrive(2, -1)
+    l_arrive(3, 1)
+    gr.arrive(-1, 0, 0)
+    gr.arrive(0, 1, 2)
+    l_arrive(1, -1)
+    gr.arrive(1, 0, 3)
+    l_arrive(3, -1)
+    gr.arrive(-1, 0, 2)
+    gr.arrive(0, 1, 3)
     finish_sum(5)
     r_begin(1)
-    finish_sum(6)
-    finish_sum(7)
-    r_begin(3)
-    l_near(3)
-    l_near(4)
-    r_near(0)
-    l_near(5)
-    r_near(2)
-    l_near(6)
-    r_near(1)
-    r_far(0)
-    r_far(2)
-    l_near(7)
-    r_near(3)
-    r_far(1)
-    r_far(3)
-    for n in range(8):
-        l_arrive(n, 2)
-    for k in range(4):
-        gr.arrive(2, 0, k)
-        gr.arrive(2, 1, k)
-    for h in range(2):
-        gx.arrive(-1, 1, h)
-        gx.arrive(1, 1, h)
+    gr.arrive(-1, 1, 0)
+    gr.arrive(1, 1, 2)
+    l_arrive(1, 1)
+    gr.arrive(0, 1, 0)
+    gr.arrive(2, 0, 0)
+    l_arrive(5, 1)
+    gr.arrive(1, 1, 3)
+    gr.arrive(1, 0, 1)
+    gr.arrive(2, 0, 3)
+    gr.arrive(-1, 1, 2)
+    l_arrive(6, -1)
+    l_arrive(4, -1)
+    l_arrive(6, 1)
+    l_arrive(7, 1)
+    l_arrive(3, 2)
+    gr.arrive(0, 1, 1)
+    gr.arrive(1, 1, 1)
+    l_arrive(4, 1)
+    gr.arrive(-1, 1, 3)
+    l_arrive(5, -1)
+    l_arrive(2, 1)
+    l_arrive(2, 2)
+    gr.arrive(-1, 0, 3)
+    gr.arrive(1, 0, 2)
+    gr.arrive(1, 0, 0)
+    l_arrive(7, -1)
+    gr.arrive(1, 1, 0)
+    l_arrive(0, 2)
+    l_arrive(5, 2)
+    l_arrive(1, 2)
+    l_arrive(6, 2)
+    l_arrive(0, 1)
+    gr.arrive(2, 0, 2)
+    l_arrive(7, 2)
+    l_arrive(4, 2)
+    gr.arrive(-1, 0, 1)
+    gr.arrive(2, 0, 1)
+    gr.arrive(2, 1, 2)
+    gr.arrive(2, 1, 0)
+    gr.arrive(2, 1, 3)
+    gr.arrive(-1, 1, 1)
+    gr.arrive(2, 1, 1)
+    gx.arrive(-1, 1, 1)
+    gx.arrive(1, 1, 0)
 
     def square(j, rows):
         left = rt[j, rows].reshape(-1, CHIP)
         right = ls[j].reshape(CHIP, CHIP)
         return jnp.dot(left, right, preferred_element_type=jnp.float32)
 
-    for n in range(8):
+    def squares(ns, rows):
+        return sum(square(chip_at(parts[n][1], parts[n][0]), rows) for n in ns)
+
+    done = ((0, 1, 2, 5), (3, 4), (6, 7))
+    for ns in done[:2]:
+        for n in ns:
+            for dz in (0, -1, 1, 2):
+                from_core(n, dz)
+        total = squares(ns, slice(None)).reshape(4, PIECE, CHIP)
+        sq[...] = total if ns == done[0] else sq[...] + total
+    for n in done[2]:
         for dz in (0, -1, 1, 2):
-            if parts[n][0] == 0:
-                from_core(n, dz)
-    for h in range(2):
-        rows = slice(2 * h, 2 * h + 2)
-        total = square(yl * 4, rows)
-        for k in range(1, 4):
-            total = total + square(yl * 4 + k, rows)
-        sq[rows] = total.reshape(2, PIECE, CHIP)
-    for n in range(8):
-        for dz in (0, -1, 1, 2):
-            if parts[n][0] == 1:
-                from_core(n, dz)
+            from_core(n, dz)
 
     def mix_slot(dr, dp, h):
         return ms.at[h, :, (yh + dp) % 2, (z + dr + 4) % 4]
@@ -371,9 +427,7 @@
     gm = Gather(mix_slot, zp, zm, yq, m_send, m_recv, "cross")
     for h in range(2):
         rows = slice(2 * h, 2 * h + 2)
-        total = sq[rows].reshape(HALF, CHIP)
-        for k in range(4):
-            total = total + square((1 - yl) * 4 + k, rows)
+        total = sq[rows].reshape(HALF, CHIP) + squares(done[2], rows)
         gram_rows = jnp.concatenate([gf[h * 4 + yh], gf[h * 4 + 2 + yh]], axis=0)
         mixing = (COEF_B * gram_rows + COEF_C * total).astype(jnp.bfloat16)
         ms[h, 0, yh, z] = mixing[:PIECE]
@@ -384,16 +438,21 @@
             gm.begin(1, ("minus", "plus", "pair"))
             gm.begin(0, ("minus",))
 
-    def turn(dr, dp, slot):
-        mt[slot] = ms[:, :, (yh + dp) % 2, (z + dr + 4) % 4].reshape(ROWS, CHIP).T
-
-    def product(dr, dp, slot, rows, n, first=False):
+    def turn(dr, dp):
+        mt[...] = ms[:, :, (yh + dp) % 2, (z + dr + 4) % 4].reshape(ROWS, CHIP).T
+
+    def product(dr, dp, rows, n, first=False):
         side, at = (yh + dp) % 2, (z + dr + 4) % 4
         cols = pl.ds(n * 384, 384)
         at_rows = pl.ds(pl.multiple_of(at * PIECE, 16), PIECE)
         right = jnp.concatenate([xs[2 * k + side, at_rows, cols] for k in range(4)], axis=0)
-        part = jnp.dot(mt[slot, rows, :], right, preferred_element_type=jnp.float32)
+        part = jnp.dot(mt[rows, :], right, preferred_element_type=jnp.float32)
         zs[rows, cols] = part if first else zs[rows, cols] + part
+
+    def unit(dr, dp, first=False):
+        turn(dr, dp)
+        for n in range(3):
+            product(dr, dp, every, n, first)
 
     every = slice(None)
     for h in range(2):
@@ -402,33 +461,31 @@
         gm.arrive(0, 1, h)
     for h in range(2):
         gx.arrive(2, 1, h)
-    turn(0, 0, 0)
-    for n in range(3):
-        product(0, 0, 0, every, n, True)
-    for h in range(2):
-        gm.arrive(-1, 1, h)
-        gm.arrive(1, 1, 1 - h)
+    unit(0, 0, True)
+    unit(-1, 0)
+    unit(1, 0)
+    gm.arrive(-1, 1, 0)
+    gm.arrive(1, 1, 1)
+    unit(0, 1)
     for h in range(2):
         gm.arrive(2, 0, h)
-    for place in near + ((2, 0),):
-        turn(*place, 0)
-        for n in range(3):
-            product(*place, 0, every, n)
-    for k, place in enumerate(far):
-        if place == (2, 1):
-            for h in range(2):
-                gm.arrive(*place, h)
-        turn(*place, k)
+    unit(2, 0)
+    gm.arrive(-1, 1, 1)
+    gm.arrive(1, 1, 0)
+    unit(-1, 1)
+    unit(1, 1)
+    for h in range(2):
+        gm.arrive(2, 1, h)
+    turn(2, 1)
     last = []
     for n in range(3):
-        for k, place in enumerate(far):
-            product(*place, k, theirs, n)
+        product(2, 1, theirs, n)
         zb[n] = zs[theirs, pl.ds(n * 384, 384)].astype(jnp.bfloat16)
         last.append(remote(zb.at[n], zr.at[n], z_send.at[n], z_recv.at[n], core))
         last[n].start()
     for n in range(3):
-        for k, place in enumerate(far):
-            product(*place, k, mine, n)
+        product(2, 1, mine, n)
+    for n in range(3):
         last[n].wait_recv()
         cols = pl.ds(n * 384, 384)
         out_ref[:, cols] = zs[mine, cols] + zr[n].astype(jnp.float32)
@@ -437,9 +494,11 @@
         copy.wait_send()
     for gather in (gx, gr, gm):
         gather.finish()
-    for block in range(8):
-        for dz in (1, 2, 3):
-            piece_copy(block, dz).wait_send()
+    for place in parts:
+        for _, copy in pieces_of(*place):
+            copy.wait_send()
+        if place in RELAY:
+            onward(*place).wait_send()
     for xj in range(4):
         for slot in range(3):
             sum_copy(min(slot, 1), xj, slot).wait_send()
@@ -461,6 +520,8 @@
             pltpu.VMEM((2, ROWS, COLS), half),
             pltpu.VMEM((2, COLS, CHIP), half),
             pltpu.VMEM((8, 4, PIECE, CHIP), half),
+            pltpu.VMEM((8, PIECE, CHIP), half),
+            pltpu.VMEM((8, PIECE, CHIP), half),
             pltpu.VMEM((8, 3, PIECE, CHIP), half),
             pltpu.VMEM((4, PIECE, CHIP), full),
             pltpu.VMEM((2, 4, PIECE, CHIP), half),
@@ -470,12 +531,12 @@
             pltpu.VMEM((8, 4, PIECE, CHIP), half),
             pltpu.VMEM((8, 2, 4, PIECE, CHIP), half),
             pltpu.VMEM((2, 2, 2, 4, PIECE, CHIP), half),
-            pltpu.VMEM((3, CHIP, ROWS), half),
+            pltpu.VMEM((CHIP, ROWS), half),
             pltpu.VMEM((CHIP, COLS), full),
             pltpu.VMEM((3, ROWS, 384), half),
             pltpu.VMEM((3, ROWS, 384), half),
             dma((4,)), dma((14,)), dma((16,)), dma(()), dma(()), dma((2,)), dma((2,)), dma((2,)),
-            dma((8, 3)), dma((8, 3)), dma((3, 4)), dma((3, 4)),
+            dma((8,)), dma((8,)), dma((8, 3)), dma((8, 3)), dma((3, 4)), dma((3, 4)),
             dma((28,)), dma((32,)), dma((28,)), dma((32,)),
             dma((32,)), dma((32,)), dma((14,)), dma((16,)),
             dma((3,)), dma((3,)),

time: 127 us -> 118 us (0.929)
  Pallas kernels: 123 us -> 114 us
    pallas_call x1, Pallas kernels: 123 us -> 114 us  [local(): pl.pallas_call(kernel, out_shape=jax.ShapeDtypeStruct((ROWS, COLS), full)...]
where the time goes in v7:
time: 118 us
  Pallas kernels  114 us (97%)
  other arithmetic  3.35 us (3%)
    pallas_call x1, Pallas kernels, local(): pl.pallas_call(kernel, out_shape=jax.ShapeDtypeStruct((ROWS, COLS), full)...  114 us
    mul x1, other arithmetic, local(): return (new_momentum, SCALE * (COEF_A * nesterov + product))  3.35 us

profile of v7, /device:TPU:1, one launch (start us, length us, event | category | flops | bytes accessed | tf_op | source)
XLA Modules:
  0.0 117.8 jit_solution(14786590070248891630)
XLA Ops:
  0.6 0.0 copy-start.1
  0.6 0.0 copy-start
  0.6 113.8 %muon.1 = f32[320,1152]{1,0:T(8,128)} custom-call(f32[320,1152]{1,0:T(8,128)} %g_hbm.1, f32[320,1152]{1,0:T(8,128)} %m_hbm.1), custom_call_target="tpu_custom_call" | custom-call | tf_op jit(solution)/shard_map/muon/pallas_call | solution.py:510
  114.5 0.0 copy-done.1
  114.5 0.0 copy-done
  114.5 3.3 %add_multiply_fusion = (f32[320,1152]{1,0:T(8,128)}, f32[320,1152]{1,0:T(8,128)}) fusion(f32[320,1152]{1,0:T(8,128)} %muon.1, f32[320,1152]{1,0:T(8,128)S(1)} %copy-done, f32[320,1152]{1,0:T(8,128)S(1)} %copy-done.1), kind=kLoop, calls=%fused_computation | loop fusion | flops 2580480 | bytes 7372800 | tf_op jit(solution)/shard_map/mul | solution.py:551
Async XLA Ops:
  0.6 113.8 %copy-start.1 = (f32[320,1152]{1,0:T(8,128)S(1)}, f32[320,1152]{1,0:T(8,128)}, u32[]{:S(2)}) copy-start(f32[320,1152]{1,0:T(8,128)} %m_hbm.1) | copy-start | bytes 4423684
  0.6 113.8 %copy-start = (f32[320,1152]{1,0:T(8,128)S(1)}, f32[320,1152]{1,0:T(8,128)}, u32[]{:S(2)}) copy-start(f32[320,1152]{1,0:T(8,128)} %g_hbm.1) | copy-start | bytes 4423684

commit v8 on v7

--- a/solution.py
+++ b/solution.py
@@ -20,7 +20,7 @@
 HALF = ROWS // 2
 CHIP = 2 * ROWS
 PIECE = ROWS // 4
-RELAY = {(0, 1): 1, (1, -1): 1, (1, 1): -1, (0, 2): 1, (1, 2): -1}
+RELAY = {(1, 0): -1, (1, -1): 1, (1, 1): -1, (0, 2): 1, (1, 2): 1}
 PLACES = {(0, 0): 0, (-1, 0): 1, (1, 0): 2, (2, 0): 3, (0, 1): 4, (-1, 1): 5, (1, 1): 6, (2, 1): 7}
 
 
@@ -56,6 +56,9 @@
             self._copy(0, 1, h, "plus")
         if self.mode != "cross" or h % 2 == 0:
             self._copy(0, 1, h, "minus")
+
+    def pass_far(self, h):
+        self._copy(2, 0, h, "pair")
 
     def arrive(self, dr, dp, h):
         ref = self.slot(dr, dp, h)
@@ -75,8 +78,6 @@
             self._copy(dr, dp, h, "plus" if dr == -1 else "minus")
             if self.mode == "cross" and dp == 0:
                 self._copy(dr, dp, h, "pair")
-        elif (dr, dp) == (2, 0) and self.mode == "late":
-            self._copy(dr, dp, h, "pair")
 
     def finish(self):
         for copy in self.started:
@@ -124,7 +125,7 @@
 
     own = chip_at(0, 0)
 
-    gx = Gather(lambda dr, dp, h: xs.at[chip_at(dr, dp), pl.ds(h * HALF, HALF)], xp, xm, yp, x_send, x_recv, "ring", hold=True)
+    gx = Gather(lambda dr, dp, h: xs.at[chip_at(dr, dp), pl.ds(h * HALF, HALF)], xp, xm, yp, x_send, x_recv, "late", hold=True)
     mine = pl.ds(pl.multiple_of(c * ROWS, 32), ROWS)
     theirs = pl.ds(pl.multiple_of((1 - c) * ROWS, 32), ROWS)
     for h in range(2):
@@ -292,115 +293,116 @@
 
     passed = []
     gram(0, 0, 1)
+    gram(0, 0, 0)
     gx.arrive(-1, 0, 0)
-    gram(0, -1, 0)
     gx.arrive(1, 0, 1)
-    gram(0, 0, 0)
-    gram(0, 1, 1)
     gx.arrive(0, 1, 0)
     passed.append(pass_pair(0))
+    gram(0, 1, 1)
+    gram(0, -1, 0)
     gx.arrive(-1, 0, 1)
     gram(0, -1, 1)
     gx.arrive(1, 0, 0)
+    reduce(0, 0)
     gx.arrive(0, 1, 1)
     passed.append(pass_pair(1))
     gram(0, 1, 0)
     load_pair()
+    gram(1, 0, 1)
+    gx.spread(1)
+    gram(1, -1, 0)
+    gram(1, -1, 1)
+    reduce(0, -1)
     gram(1, 0, 0)
-    gx.spread(1)
+    gx.arrive(2, 0, 1)
+    gx.arrive(2, 0, 0)
     gram(1, 1, 1)
-    gram(1, -1, 1)
-    gram(1, 0, 1)
-    reduce(0, 0)
-    gx.arrive(2, 0, 0)
-    gram(1, -1, 0)
-    gx.arrive(2, 0, 1)
+    gx.pass_far(1)
+    gram(1, 1, 0)
+    reduce(0, 1)
+    relay(1, -1)
+    gram(1, 2, 1)
+    relay(1, 0)
     gx.spread(0)
-    relay(0, 1)
+    relay(1, 1)
+    gram(1, 2, 0)
+    finish_sum(1)
+    reduce(1, -1)
+    relay(1, 2)
+    gram(0, 2, 1)
+    reduce(1, 0)
     gram(0, 2, 0)
-    gram(0, 2, 1)
-    gram(1, 2, 1)
-    reduce(0, -1)
-    gram(1, 1, 0)
-    relay(1, -1)
-    gram(1, 2, 0)
-    reduce(1, 0)
-    reduce(0, 1)
     finish_sum(0)
-    relay(1, 2)
-    relay(1, 1)
-    gx.arrive(1, 1, 1)
+    r_begin(0)
+    reduce(1, 1)
+    l_arrive(1, 1)
+    finish_sum(4)
     relay(0, 2)
-    finish_sum(1)
-    r_begin(0)
-    gx.arrive(-1, 1, 0)
-    reduce(1, -1)
+    reduce(1, 2)
+    gr.arrive(-1, 0, 0)
+    finish_sum(3)
     finish_sum(2)
-    finish_sum(3)
-    reduce(1, 2)
-    reduce(1, 1)
-    finish_sum(4)
     r_begin(2)
+    finish_sum(6)
     reduce(0, 2)
-    finish_sum(6)
+    gr.arrive(0, 1, 0)
+    l_arrive(4, 1)
     finish_sum(7)
+    r_begin(3)
+    gr.arrive(-1, 1, 0)
+    l_arrive(2, 1)
+    gr.arrive(0, 1, 2)
+    gr.arrive(-1, 0, 2)
+    l_arrive(2, -1)
+    l_arrive(1, -1)
+    gr.arrive(1, 0, 0)
+    gr.arrive(2, 0, 0)
+    finish_sum(5)
     l_arrive(0, -1)
-    r_begin(3)
-    l_arrive(2, -1)
+    l_arrive(0, 1)
+    r_begin(1)
+    l_arrive(4, -1)
+    gr.arrive(1, 0, 2)
+    l_arrive(7, 1)
+    l_arrive(3, -1)
+    gr.arrive(1, 0, 3)
+    l_arrive(6, -1)
+    l_arrive(5, 1)
+    l_arrive(7, -1)
+    gr.arrive(1, 0, 1)
+    gr.arrive(0, 1, 3)
+    gr.arrive(-1, 0, 3)
+    gx.pass_far(0)
     l_arrive(3, 1)
-    gr.arrive(-1, 0, 0)
-    gr.arrive(0, 1, 2)
-    l_arrive(1, -1)
-    gr.arrive(1, 0, 3)
-    l_arrive(3, -1)
-    gr.arrive(-1, 0, 2)
-    gr.arrive(0, 1, 3)
-    finish_sum(5)
-    r_begin(1)
-    gr.arrive(-1, 1, 0)
     gr.arrive(1, 1, 2)
-    l_arrive(1, 1)
-    gr.arrive(0, 1, 0)
-    gr.arrive(2, 0, 0)
-    l_arrive(5, 1)
+    l_arrive(7, 2)
+    gr.arrive(-1, 0, 1)
+    gr.arrive(-1, 1, 2)
     gr.arrive(1, 1, 3)
-    gr.arrive(1, 0, 1)
-    gr.arrive(2, 0, 3)
-    gr.arrive(-1, 1, 2)
-    l_arrive(6, -1)
-    l_arrive(4, -1)
-    l_arrive(6, 1)
-    l_arrive(7, 1)
-    l_arrive(3, 2)
+    gr.arrive(2, 0, 1)
+    l_arrive(5, 2)
     gr.arrive(0, 1, 1)
     gr.arrive(1, 1, 1)
-    l_arrive(4, 1)
+    l_arrive(2, 2)
+    l_arrive(1, 2)
+    gr.arrive(2, 1, 2)
+    gr.arrive(1, 1, 0)
+    l_arrive(3, 2)
+    gr.arrive(2, 1, 0)
+    l_arrive(4, 2)
+    l_arrive(5, -1)
+    l_arrive(6, 1)
+    l_arrive(0, 2)
+    gr.arrive(2, 0, 3)
+    l_arrive(6, 2)
     gr.arrive(-1, 1, 3)
-    l_arrive(5, -1)
-    l_arrive(2, 1)
-    l_arrive(2, 2)
-    gr.arrive(-1, 0, 3)
-    gr.arrive(1, 0, 2)
-    gr.arrive(1, 0, 0)
-    l_arrive(7, -1)
-    gr.arrive(1, 1, 0)
-    l_arrive(0, 2)
-    l_arrive(5, 2)
-    l_arrive(1, 2)
-    l_arrive(6, 2)
-    l_arrive(0, 1)
-    gr.arrive(2, 0, 2)
-    l_arrive(7, 2)
-    l_arrive(4, 2)
-    gr.arrive(-1, 0, 1)
-    gr.arrive(2, 0, 1)
-    gr.arrive(2, 1, 2)
-    gr.arrive(2, 1, 0)
     gr.arrive(2, 1, 3)
     gr.arrive(-1, 1, 1)
+    gr.arrive(2, 0, 2)
     gr.arrive(2, 1, 1)
-    gx.arrive(-1, 1, 1)
-    gx.arrive(1, 1, 0)
+    for h in range(2):
+        gx.arrive(-1, 1, h)
+        gx.arrive(1, 1, h)
 
     def square(j, rows):
         left = rt[j, rows].reshape(-1, CHIP)
@@ -543,7 +545,7 @@
         ],
         name="muon",
         compiler_params=pltpu.CompilerParams(
-            collective_id=0, has_side_effects=True, vmem_limit_bytes=60 * 2**20
+            collective_id=0, has_side_effects=True, vmem_limit_bytes=52 * 2**20
         ),
     )(gradient, momentum)
     new_momentum = MOMENTUM_RATE * momentum + gradient

time: 118 us -> 116 us (0.983)
  other arithmetic: 3.35 us -> 1.98 us
    mul x1, other arithmetic: 3.35 us -> 1.98 us  [local(): return (new_momentum, SCALE * (COEF_A * nesterov + product))]
where the time goes in v8:
time: 116 us
  Pallas kernels  113 us (97%)
  other arithmetic  1.98 us (2%)
    pallas_call x1, Pallas kernels, local(): pl.pallas_call(kernel, out_shape=jax.ShapeDtypeStruct((ROWS, COLS), full)...  113 us

profile of v8, /device:TPU:1, one launch (start us, length us, event | category | flops | bytes accessed | tf_op | source)
XLA Modules:
  0.0 115.7 jit_solution(15469932111530829818)
XLA Ops:
  0.6 0.0 copy-start.1
  0.6 0.0 copy-start
  0.6 113.0 %muon.1 = f32[320,1152]{1,0:T(8,128)S(1)} custom-call(f32[320,1152]{1,0:T(8,128)} %g_hbm.1, f32[320,1152]{1,0:T(8,128)} %m_hbm.1), custom_call_target="tpu_custom_call" | custom-call | tf_op jit(solution)/shard_map/muon/pallas_call | solution.py:512
  113.7 0.0 copy-done.1
  113.7 0.0 copy-done
  113.7 2.0 %add_multiply_fusion = (f32[320,1152]{1,0:T(8,128)}, f32[320,1152]{1,0:T(8,128)}) fusion(f32[320,1152]{1,0:T(8,128)S(1)} %muon.1, f32[320,1152]{1,0:T(8,128)S(1)} %copy-done, f32[320,1152]{1,0:T(8,128)S(1)} %copy-done.1), kind=kLoop, calls=%fused_computation | loop fusion | flops 2580480 | bytes 7372800 | tf_op jit(solution)/shard_map/mul | solution.py:553
Async XLA Ops:
  0.6 113.1 %copy-start.1 = (f32[320,1152]{1,0:T(8,128)S(1)}, f32[320,1152]{1,0:T(8,128)}, u32[]{:S(2)}) copy-start(f32[320,1152]{1,0:T(8,128)} %m_hbm.1) | copy-start | bytes 4423684
  0.6 113.1 %copy-start = (f32[320,1152]{1,0:T(8,128)S(1)}, f32[320,1152]{1,0:T(8,128)}, u32[]{:S(2)}) copy-start(f32[320,1152]{1,0:T(8,128)} %g_hbm.1) | copy-start | bytes 4423684

commit v9 on v8

--- a/solution.py
+++ b/solution.py
@@ -20,7 +20,7 @@
 HALF = ROWS // 2
 CHIP = 2 * ROWS
 PIECE = ROWS // 4
-RELAY = {(1, 0): -1, (1, -1): 1, (1, 1): -1, (0, 2): 1, (1, 2): 1}
+RELAY = {(1, 0): -1, (1, -1): -1, (1, 1): -1, (0, 2): 1, (1, 2): 1}
 PLACES = {(0, 0): 0, (-1, 0): 1, (1, 0): 2, (2, 0): 3, (0, 1): 4, (-1, 1): 5, (1, 1): 6, (2, 1): 7}
 
 
@@ -291,119 +291,6 @@
             cols = slice(k * 128, (k + 1) * 128)
             xt[1, cols, :] = xq[:, :, cols].reshape(CHIP, 128).T
 
-    passed = []
-    gram(0, 0, 1)
-    gram(0, 0, 0)
-    gx.arrive(-1, 0, 0)
-    gx.arrive(1, 0, 1)
-    gx.arrive(0, 1, 0)
-    passed.append(pass_pair(0))
-    gram(0, 1, 1)
-    gram(0, -1, 0)
-    gx.arrive(-1, 0, 1)
-    gram(0, -1, 1)
-    gx.arrive(1, 0, 0)
-    reduce(0, 0)
-    gx.arrive(0, 1, 1)
-    passed.append(pass_pair(1))
-    gram(0, 1, 0)
-    load_pair()
-    gram(1, 0, 1)
-    gx.spread(1)
-    gram(1, -1, 0)
-    gram(1, -1, 1)
-    reduce(0, -1)
-    gram(1, 0, 0)
-    gx.arrive(2, 0, 1)
-    gx.arrive(2, 0, 0)
-    gram(1, 1, 1)
-    gx.pass_far(1)
-    gram(1, 1, 0)
-    reduce(0, 1)
-    relay(1, -1)
-    gram(1, 2, 1)
-    relay(1, 0)
-    gx.spread(0)
-    relay(1, 1)
-    gram(1, 2, 0)
-    finish_sum(1)
-    reduce(1, -1)
-    relay(1, 2)
-    gram(0, 2, 1)
-    reduce(1, 0)
-    gram(0, 2, 0)
-    finish_sum(0)
-    r_begin(0)
-    reduce(1, 1)
-    l_arrive(1, 1)
-    finish_sum(4)
-    relay(0, 2)
-    reduce(1, 2)
-    gr.arrive(-1, 0, 0)
-    finish_sum(3)
-    finish_sum(2)
-    r_begin(2)
-    finish_sum(6)
-    reduce(0, 2)
-    gr.arrive(0, 1, 0)
-    l_arrive(4, 1)
-    finish_sum(7)
-    r_begin(3)
-    gr.arrive(-1, 1, 0)
-    l_arrive(2, 1)
-    gr.arrive(0, 1, 2)
-    gr.arrive(-1, 0, 2)
-    l_arrive(2, -1)
-    l_arrive(1, -1)
-    gr.arrive(1, 0, 0)
-    gr.arrive(2, 0, 0)
-    finish_sum(5)
-    l_arrive(0, -1)
-    l_arrive(0, 1)
-    r_begin(1)
-    l_arrive(4, -1)
-    gr.arrive(1, 0, 2)
-    l_arrive(7, 1)
-    l_arrive(3, -1)
-    gr.arrive(1, 0, 3)
-    l_arrive(6, -1)
-    l_arrive(5, 1)
-    l_arrive(7, -1)
-    gr.arrive(1, 0, 1)
-    gr.arrive(0, 1, 3)
-    gr.arrive(-1, 0, 3)
-    gx.pass_far(0)
-    l_arrive(3, 1)
-    gr.arrive(1, 1, 2)
-    l_arrive(7, 2)
-    gr.arrive(-1, 0, 1)
-    gr.arrive(-1, 1, 2)
-    gr.arrive(1, 1, 3)
-    gr.arrive(2, 0, 1)
-    l_arrive(5, 2)
-    gr.arrive(0, 1, 1)
-    gr.arrive(1, 1, 1)
-    l_arrive(2, 2)
-    l_arrive(1, 2)
-    gr.arrive(2, 1, 2)
-    gr.arrive(1, 1, 0)
-    l_arrive(3, 2)
-    gr.arrive(2, 1, 0)
-    l_arrive(4, 2)
-    l_arrive(5, -1)
-    l_arrive(6, 1)
-    l_arrive(0, 2)
-    gr.arrive(2, 0, 3)
-    l_arrive(6, 2)
-    gr.arrive(-1, 1, 3)
-    gr.arrive(2, 1, 3)
-    gr.arrive(-1, 1, 1)
-    gr.arrive(2, 0, 2)
-    gr.arrive(2, 1, 1)
-    for h in range(2):
-        gx.arrive(-1, 1, h)
-        gx.arrive(1, 1, h)
-
     def square(j, rows):
         left = rt[j, rows].reshape(-1, CHIP)
         right = ls[j].reshape(CHIP, CHIP)
@@ -412,16 +299,135 @@
     def squares(ns, rows):
         return sum(square(chip_at(parts[n][1], parts[n][0]), rows) for n in ns)
 
-    done = ((0, 1, 2, 5), (3, 4), (6, 7))
-    for ns in done[:2]:
-        for n in ns:
-            for dz in (0, -1, 1, 2):
-                from_core(n, dz)
-        total = squares(ns, slice(None)).reshape(4, PIECE, CHIP)
-        sq[...] = total if ns == done[0] else sq[...] + total
-    for n in done[2]:
+    def square_add(n, first=False):
         for dz in (0, -1, 1, 2):
             from_core(n, dz)
+        total = squares((n,), slice(None)).reshape(4, PIECE, CHIP)
+        sq[...] = total if first else sq[...] + total
+
+    passed = []
+    gram(0, 0, 1)
+    gx.arrive(1, 0, 1)
+    gx.arrive(-1, 0, 0)
+    gram(0, -1, 0)
+    gx.arrive(0, 1, 0)
+    passed.append(pass_pair(0))
+    gram(0, 1, 1)
+    gram(0, 0, 0)
+    gx.arrive(0, 1, 1)
+    passed.append(pass_pair(1))
+    gx.arrive(-1, 0, 1)
+    gram(0, -1, 1)
+    gx.spread(1)
+    gx.arrive(1, 0, 0)
+    gram(0, 1, 0)
+    load_pair()
+    reduce(0, 0)
+    gram(1, -1, 0)
+    gram(1, 1, 1)
+    gram(1, 0, 1)
+    gram(1, -1, 1)
+    reduce(0, -1)
+    gx.arrive(2, 0, 1)
+    gram(1, 1, 0)
+    gx.pass_far(1)
+    gram(1, 0, 0)
+    relay(1, -1)
+    reduce(0, 1)
+    gx.arrive(2, 0, 0)
+    gram(1, 2, 0)
+    finish_sum(1)
+    relay(1, 0)
+    gram(0, 2, 1)
+    relay(1, 1)
+    gram(1, 2, 1)
+    finish_sum(0)
+    r_begin(0)
+    gram(0, 2, 0)
+    reduce(1, -1)
+    gr.arrive(-1, 0, 0)
+    gx.spread(0)
+    relay(1, 2)
+    finish_sum(2)
+    reduce(1, 0)
+    gr.arrive(0, 1, 0)
+    reduce(1, 1)
+    relay(0, 2)
+    reduce(1, 2)
+    finish_sum(4)
+    finish_sum(3)
+    r_begin(2)
+    l_arrive(1, -1)
+    finish_sum(6)
+    l_arrive(2, -1)
+    reduce(0, 2)
+    l_arrive(4, -1)
+    l_arrive(0, -1)
+    gr.arrive(-1, 0, 2)
+    finish_sum(7)
+    r_begin(3)
+    l_arrive(0, 1)
+    gr.arrive(1, 0, 0)
+    finish_sum(5)
+    r_begin(1)
+    l_arrive(3, 1)
+    l_arrive(1, 1)
+    l_arrive(2, 1)
+    gr.arrive(0, 1, 2)
+    l_arrive(3, -1)
+    gr.arrive(-1, 1, 0)
+    gr.arrive(1, 0, 3)
+    l_arrive(6, -1)
+    l_arrive(5, 1)
+    gr.arrive(0, 1, 1)
+    gr.arrive(1, 0, 1)
+    l_arrive(7, 1)
+    gr.arrive(2, 0, 2)
+    gr.arrive(-1, 0, 1)
+    gr.arrive(1, 1, 2)
+    gr.arrive(-1, 0, 3)
+    gx.pass_far(0)
+    l_arrive(3, 2)
+    l_arrive(4, 2)
+    l_arrive(0, 2)
+    gr.arrive(1, 1, 3)
+    gr.arrive(-1, 1, 2)
+    l_arrive(2, 2)
+    l_arrive(4, 1)
+    l_arrive(1, 2)
+    gr.arrive(0, 1, 3)
+    gr.arrive(1, 1, 1)
+    gr.arrive(2, 0, 0)
+    square_add(0, True)
+    l_arrive(5, -1)
+    square_add(3)
+    square_add(1)
+    l_arrive(5, 2)
+    gr.arrive(2, 1, 0)
+    l_arrive(6, 1)
+    l_arrive(6, 2)
+    gr.arrive(1, 0, 2)
+    gr.arrive(1, 1, 0)
+    gr.arrive(2, 0, 1)
+    gr.arrive(2, 1, 2)
+    square_add(2)
+    l_arrive(7, 2)
+    gr.arrive(2, 1, 3)
+    gr.arrive(2, 0, 3)
+    l_arrive(7, -1)
+    square_add(5)
+    gr.arrive(-1, 1, 1)
+    gr.arrive(-1, 1, 3)
+    square_add(6)
+    gr.arrive(2, 1, 1)
+    for h in range(2):
+        gx.arrive(-1, 1, h)
+        gx.arrive(1, 1, h)
+
+    done = (4, 7)
+    for n in done:
+        for dz in (0, -1, 1, 2):
+            from_core(n, dz)
 
     def mix_slot(dr, dp, h):
         return ms.at[h, :, (yh + dp) % 2, (z + dr + 4) % 4]
@@ -429,7 +435,7 @@
     gm = Gather(mix_slot, zp, zm, yq, m_send, m_recv, "cross")
     for h in range(2):
         rows = slice(2 * h, 2 * h + 2)
-        total = sq[rows].reshape(HALF, CHIP) + squares(done[2], rows)
+        total = sq[rows].reshape(HALF, CHIP) + squares(done, rows)
         gram_rows = jnp.concatenate([gf[h * 4 + yh], gf[h * 4 + 2 + yh]], axis=0)
         mixing = (COEF_B * gram_rows + COEF_C * total).astype(jnp.bfloat16)
         ms[h, 0, yh, z] = mixing[:PIECE]

time: 116 us -> 115 us (level)
  no operation moved by 1% of the time
where the time goes in v9:
time: 115 us
  Pallas kernels  112 us (97%)
  other arithmetic  1.98 us (2%)
    pallas_call x1, Pallas kernels, local(): pl.pallas_call(kernel, out_shape=jax.ShapeDtypeStruct((ROWS, COLS), full)...  112 us

profile of v9, /device:TPU:1, one launch (start us, length us, event | category | flops | bytes accessed | tf_op | source)
XLA Modules:
  0.0 115.0 jit_solution(8810245286553864533)
XLA Ops:
  0.6 0.0 copy-start.1
  0.6 0.0 copy-start
  0.6 112.3 %muon.1 = f32[320,1152]{1,0:T(8,128)S(1)} custom-call(f32[320,1152]{1,0:T(8,128)} %g_hbm.1, f32[320,1152]{1,0:T(8,128)} %m_hbm.1), custom_call_target="tpu_custom_call" | custom-call | tf_op jit(solution)/shard_map/muon/pallas_call | solution.py:518
  113.0 0.0 copy-done.1
  113.0 0.0 copy-done
  113.0 2.0 %add_multiply_fusion = (f32[320,1152]{1,0:T(8,128)}, f32[320,1152]{1,0:T(8,128)}) fusion(f32[320,1152]{1,0:T(8,128)S(1)} %muon.1, f32[320,1152]{1,0:T(8,128)S(1)} %copy-done, f32[320,1152]{1,0:T(8,128)S(1)} %copy-done.1), kind=kLoop, calls=%fused_computation | loop fusion | flops 2580480 | bytes 7372800 | tf_op jit(solution)/shard_map/mul | solution.py:559
Async XLA Ops:
  0.6 112.3 %copy-start.1 = (f32[320,1152]{1,0:T(8,128)S(1)}, f32[320,1152]{1,0:T(8,128)}, u32[]{:S(2)}) copy-start(f32[320,1152]{1,0:T(8,128)} %m_hbm.1) | copy-start | bytes 4423684
  0.6 112.3 %copy-start = (f32[320,1152]{1,0:T(8,128)S(1)}, f32[320,1152]{1,0:T(8,128)}, u32[]{:S(2)}) copy-start(f32[320,1152]{1,0:T(8,128)} %g_hbm.1) | copy-start | bytes 4423684

commit v10 on v9

--- a/solution.py
+++ b/solution.py
@@ -105,8 +105,6 @@
     yd = device(x, 1 - yl, c, 1 - yh, z)
     barrier = pltpu.get_barrier_semaphore()
     partners = (core, xp, xm, zp, zm, z2, yp, yq, yd)
-    for partner in partners:
-        pl.semaphore_signal(barrier, inc=1, device_id=partner, device_id_type=MESH)
     loads = []
     for h in range(2):
         rows = pl.ds(h * HALF, HALF)
@@ -114,6 +112,8 @@
             load = pltpu.make_async_copy(hbm.at[rows], ref.at[rows], in_sem.at[2 * h + k])
             load.start()
             loads.append(load)
+    for partner in partners:
+        pl.semaphore_signal(barrier, inc=1, device_id=partner, device_id_type=MESH)
 
     def remote(src, dst, send, recv, to):
         return pltpu.make_async_remote_copy(

time: 115 us -> 115 us (level)
  no operation moved by 1% of the time
where the time goes in v10:
time: 115 us
  Pallas kernels  112 us (97%)
  other arithmetic  1.98 us (2%)
    pallas_call x1, Pallas kernels, local(): pl.pallas_call(kernel, out_shape=jax.ShapeDtypeStruct((ROWS, COLS), full)...  112 us

profile of v10, /device:TPU:1, one launch (start us, length us, event | category | flops | bytes accessed | tf_op | source)
XLA Modules:
  0.0 114.9 jit_solution(15348609032229515349)
XLA Ops:
  0.6 0.0 copy-start.1
  0.6 0.0 copy-start
  0.6 112.3 %muon.1 = f32[320,1152]{1,0:T(8,128)S(1)} custom-call(f32[320,1152]{1,0:T(8,128)} %g_hbm.1, f32[320,1152]{1,0:T(8,128)} %m_hbm.1), custom_call_target="tpu_custom_call" | custom-call | tf_op jit(solution)/shard_map/muon/pallas_call | solution.py:518
  112.9 0.0 copy-done.1
  113.0 0.0 copy-done
  113.0 2.0 %add_multiply_fusion = (f32[320,1152]{1,0:T(8,128)}, f32[320,1152]{1,0:T(8,128)}) fusion(f32[320,1152]{1,0:T(8,128)S(1)} %muon.1, f32[320,1152]{1,0:T(8,128)S(1)} %copy-done, f32[320,1152]{1,0:T(8,128)S(1)} %copy-done.1), kind=kLoop, calls=%fused_computation | loop fusion | flops 2580480 | bytes 7372800 | tf_op jit(solution)/shard_map/mul | solution.py:559
Async XLA Ops:
  0.6 112.3 %copy-start.1 = (f32[320,1152]{1,0:T(8,128)S(1)}, f32[320,1152]{1,0:T(8,128)}, u32[]{:S(2)}) copy-start(f32[320,1152]{1,0:T(8,128)} %m_hbm.1) | copy-start | bytes 4423684
  0.6 112.3 %copy-start = (f32[320,1152]{1,0:T(8,128)S(1)}, f32[320,1152]{1,0:T(8,128)}, u32[]{:S(2)}) copy-start(f32[320,1152]{1,0:T(8,128)} %g_hbm.1) | copy-start | bytes 4423684

commit v11 on v10

--- a/solution.py
+++ b/solution.py
@@ -440,11 +440,7 @@
         mixing = (COEF_B * gram_rows + COEF_C * total).astype(jnp.bfloat16)
         ms[h, 0, yh, z] = mixing[:PIECE]
         ms[h, 1, yh, z] = mixing[PIECE:]
-        if h == 0:
-            gm.begin(0, ("plus", "pair"))
-        else:
-            gm.begin(1, ("minus", "plus", "pair"))
-            gm.begin(0, ("minus",))
+        gm.begin(h)
 
     def turn(dr, dp):
         mt[...] = ms[:, :, (yh + dp) % 2, (z + dr + 4) % 4].reshape(ROWS, CHIP).T

time: 115 us -> 115 us (level)
  no operation moved by 1% of the time
where the time goes in v11:
time: 115 us
  Pallas kernels  112 us (97%)
  other arithmetic  1.98 us (2%)
    pallas_call x1, Pallas kernels, local(): pl.pallas_call(kernel, out_shape=jax.ShapeDtypeStruct((ROWS, COLS), full)...  112 us

profile of v11, /device:TPU:1, one launch (start us, length us, event | category | flops | bytes accessed | tf_op | source)
XLA Modules:
  0.0 114.9 jit_solution(8524884485546632437)
XLA Ops:
  0.6 0.0 copy-start.1
  0.6 0.0 copy-start
  0.6 112.3 %muon.1 = f32[320,1152]{1,0:T(8,128)S(1)} custom-call(f32[320,1152]{1,0:T(8,128)} %g_hbm.1, f32[320,1152]{1,0:T(8,128)} %m_hbm.1), custom_call_target="tpu_custom_call" | custom-call | tf_op jit(solution)/shard_map/muon/pallas_call | solution.py:514
  112.9 0.0 copy-done.1
  113.0 0.0 copy-done
  113.0 2.0 %add_multiply_fusion = (f32[320,1152]{1,0:T(8,128)}, f32[320,1152]{1,0:T(8,128)}) fusion(f32[320,1152]{1,0:T(8,128)S(1)} %muon.1, f32[320,1152]{1,0:T(8,128)S(1)} %copy-done, f32[320,1152]{1,0:T(8,128)S(1)} %copy-done.1), kind=kLoop, calls=%fused_computation | loop fusion | flops 2580480 | bytes 7372800 | tf_op jit(solution)/shard_map/mul | solution.py:555
Async XLA Ops:
  0.6 112.3 %copy-start.1 = (f32[320,1152]{1,0:T(8,128)S(1)}, f32[320,1152]{1,0:T(8,128)}, u32[]{:S(2)}) copy-start(f32[320,1152]{1,0:T(8,128)} %m_hbm.1) | copy-start | bytes 4423684
  0.6 112.3 %copy-start = (f32[320,1152]{1,0:T(8,128)S(1)}, f32[320,1152]{1,0:T(8,128)}, u32[]{:S(2)}) copy-start(f32[320,1152]{1,0:T(8,128)} %g_hbm.1) | copy-start | bytes 4423684
